TPU v7x, 512 devices: a whole 4x4x16 slice. The times are simulated.
512 devices in a mesh: section: 4 (over x), shard: 128 (over y, z, core).
Axes of the slice: x: 4, y: 4, z: 16, core: 2. Of those that a mesh axis runs over, the one named last changes fastest.
Arguments:
- memory: bfloat16 [131072, 512], P('shard'), may hold values from -6 to 6
- messages: bfloat16 [2, 128, 128, 4, 512], P(None, 'shard', None, 'section'), may hold values from -6 to 6
- slot_rows: int32 [2, 128, 128, 4], P(None, 'shard', None, 'section'), may hold values from 0 to 1023, as said below
- counts: int32 [2, 128, 128], P(None, 'shard'), may hold values from 0 to 4, as said below
- src_slot: int32 [2, 65536], P(None, ('section', 'shard')), may hold values from 0 to 127
- nbr_slots: int32 [2, 65536, 10], P(None, ('section', 'shard')), may hold values from 0 to 127
- time_gap: float32 [2, 65536, 10], P(None, ('section', 'shard')), may hold values from 0.1 to 100
- time_freq: float32 [128], replicated, may hold values from 0.01 to 1
- time_phase: float32 [128], replicated, may hold values from -3.140625 to 3.140625
- gru_input: bfloat16 [512, 1536], P('section'), may hold values from -0.25 to 0.25
- gru_hidden: bfloat16 [512, 1536], P('section'), may hold values from -0.25 to 0.25
- gru_bias: float32 [2, 1536], replicated, may hold values from -3 to 3
- attn_qkv: bfloat16 [512, 1536], P('section'), may hold values from -0.25 to 0.25
- attn_out: bfloat16 [512, 512], P('section'), may hold values from -0.25 to 0.25
- time_proj: bfloat16 [128, 1024], P('section'), may hold values from -0.5 to 0.5
Outputs:
- memory_out: bfloat16 [131072, 512], P('shard')
- embeddings: bfloat16 [2, 65536, 512], P(None, ('section', 'shard'))
Inputs may be any that keep to these rules, and one draw needn't show every extreme that they name: `slot_rows`: within one batch the rows of one owner named by all devices' slots are distinct. `counts`: in every batch one owner receives 4 live slots from every device.
All inputs are finite; a program needn't handle non-finite values.
Results may differ from a plain program's by a relative error of at most 0.015.
Values may be sent and summed in bfloat16 or wider, within the bound.
No kernel may reach another device: no remote copies, remote signals or barrier semaphores. Data moves between devices by JAX's collectives and lax.ppermute only.
A program may use at most 128 MiB of HBM per device.

v0:
```python
import functools
import math

import jax
import jax.numpy as jnp
from jax import lax
from jax.experimental import pallas as pl
from jax.experimental.pallas import tpu as pltpu
from jax.sharding import PartitionSpec as P

HEADS = 2
HD = 256
BATCHES = 2
NBR = 10
F = 512
TE = 128
G = 3 * F
DIGIT = 32
EXTRA = 16
HALF = 2688
BF = jnp.bfloat16
F32 = jnp.float32
VMEM_LIMIT = 40 * 2**20

VSPEC = pl.BlockSpec(memory_space=pltpu.VMEM)
ASPEC = pl.BlockSpec(memory_space=pl.ANY)
SSPEC = pl.BlockSpec(memory_space=pltpu.SMEM)
PARAMS = pltpu.CompilerParams(vmem_limit_bytes=VMEM_LIMIT)


def dot(a, b):
    return jnp.dot(a, b, preferred_element_type=F32)


def dot_nt(a, b):
    return lax.dot_general(a, b, (((1,), (1,)), ((), ())), preferred_element_type=F32)


def dot_tn(a, b):
    return lax.dot_general(a, b, (((0,), (0,)), ((), ())), preferred_element_type=F32)


def split(x):
    high = x.astype(BF)
    return high, (x - high.astype(F32)).astype(BF)


def iota(shape, dim):
    return lax.broadcasted_iota(jnp.int32, shape, dim)


def hot(mask):
    return jnp.where(mask, 1.0, 0.0).astype(BF)


TWO_PI_HIGH = 6.28125
TWO_PI_LOW = 2.0 * math.pi - TWO_PI_HIGH
SERIES = [(-1.0) ** k / math.factorial(2 * k) for k in range(9)]


def cosine(x):
    turns = jnp.round(x * (1.0 / (2.0 * math.pi)))
    r = (x - turns * TWO_PI_HIGH) - turns * TWO_PI_LOW
    s = r * r
    y = jnp.full_like(s, SERIES[8])
    for k in range(7, -1, -1):
        y = y * s + SERIES[k]
    return y


def encode_kernel(gap, freq, phase, te):
    for b in range(BATCHES):
        for n in range(NBR):
            te[b, n] = cosine(freq[...] * gap[b, n : n + 1, :] + phase[...]).astype(BF)


def place_kernel(pos, mine, other, w_in, w_hid, w_qkv, w_out, w_time, sems):
    section = pos[1]

    def copies(first, second):
        found = []
        for j in range(4):
            at = pl.multiple_of(((section - j + 4) % 4) * 128, 128)
            rows = pl.ds(at, 128)
            found += [
                (first.at[j, :, pl.ds(0, G)], w_in.at[rows, :]),
                (second.at[j, :, pl.ds(0, G)], w_hid.at[rows, :]),
                (first.at[j, :, pl.ds(G, 1152)], w_qkv.at[rows, pl.ds(0, 1152)]),
                (second.at[j, :, pl.ds(G, 384)], w_qkv.at[rows, pl.ds(1152, 384)]),
                (second.at[j, :, pl.ds(1920, F)], w_out.at[rows, :]),
            ]
            time_rows = pl.ds(pl.multiple_of(((section - j + 4) % 4) * 32, 32), 32)
            for q in range(4):
                found.append(
                    (
                        second.at[j, pl.ds(32 * q, 32), pl.ds(2432, 256)],
                        w_time.at[time_rows, pl.ds(256 * q, 256)],
                    )
                )
        return found

    def move(first, second):
        started = []
        for i, (source, target) in enumerate(copies(first, second)):
            copy = pltpu.make_async_copy(source, target, sems.at[i])
            copy.start()
            started.append(copy)
        for copy in started:
            copy.wait()

    @pl.when(pos[0] == 0)
    def _():
        move(mine, other)

    @pl.when(pos[0] != 0)
    def _():
        move(other, mine)


def gates(gx, gh, h):
    reset = jax.nn.sigmoid(gx[:, :F] + gh[:, :F])
    update = jax.nn.sigmoid(gx[:, F : 2 * F] + gh[:, F : 2 * F])
    fresh = jnp.tanh(gx[:, 2 * F :] + reset * gh[:, 2 * F :])
    return ((1.0 - update) * fresh + update * h.astype(F32)).astype(BF)


def first_kernel(recv, memory, w_in, w_hid, bias, up, gx1, base):
    slots = recv.shape[0]
    rows = memory.shape[0]
    digits = recv[:, 2 * F : 2 * F + 128].astype(F32)
    up[slots:, :] = jnp.zeros((EXTRA, F), BF)
    up[slots:, :slots] = digits.T[:EXTRA, :].astype(BF)
    number = iota((slots, rows), 1).astype(F32)
    hot0 = hot(number == digits[:, 0:1] * DIGIT + digits[:, 1:2])
    hot1 = hot(number == digits[:, 2:3] * DIGIT + digits[:, 3:4])
    got = dot(jnp.concatenate([hot0, hot1], axis=0), memory[...]).astype(BF)
    base[...] = got[slots:]
    sent = jnp.concatenate([recv[:, :F], recv[:, F : 2 * F]], axis=0)
    gx = dot(sent, w_in[...]) + bias[0:1, :]
    gx1[...] = gx[slots:]
    h = got[:slots]
    gh = dot(h, w_hid[...]) + bias[1:2, :]
    up[:slots, :] = gates(gx[:slots], gh, h)


def numbers(ups, batch, slots):
    parts = []
    for t in range(ups.shape[0] // (slots + EXTRA)):
        at = t * (slots + EXTRA) + slots
        pair = ups[at : at + EXTRA, :slots].astype(F32)
        parts.append(pair[2 * batch : 2 * batch + 1] * DIGIT + pair[2 * batch + 1 : 2 * batch + 2])
    return jnp.concatenate(parts, axis=1)


def values(ups, slots):
    parts = []
    for t in range(ups.shape[0] // (slots + EXTRA)):
        at = t * (slots + EXTRA)
        parts.append(ups[at : at + slots, :])
    return jnp.concatenate(parts, axis=0)


def second_kernel(dead, recv, ups, gx1, base, w_hid, bias, up):
    slots = recv.shape[0]
    digits = recv[:, 2 * F : 2 * F + 128].astype(F32)
    mine = digits[:, 2:3] * DIGIT + digits[:, 3:4]
    same = (numbers(ups, 0, slots) == mine) & (mine < dead)
    any_same = jnp.max(jnp.where(same, 1.0, 0.0), axis=1, keepdims=True)
    moved = dot(hot(same), values(ups, slots))
    h = jnp.where(any_same > 0.0, moved, base[...].astype(F32)).astype(BF)
    gh = dot(h, w_hid[...]) + bias[1:2, :]
    up[...] = gates(gx1[...], gh, h)


def store_kernel(memory, ups0, ups1, out):
    block = memory.shape[0]
    slots = ups0.shape[0] // (ups1.shape[0] // 128) - EXTRA
    number = (iota((block, 1), 0) + pl.program_id(0) * block).astype(F32)
    hot0 = hot(numbers(ups0, 0, slots) == number)
    hot1 = hot(numbers(ups0, 1, slots) == number)
    ones = jnp.ones((hot0.shape[1], 128), BF)
    seen0, seen1 = dot(hot0, ones), dot(hot1, ones)
    new0 = dot(hot0, values(ups0, slots))
    new1 = dot(hot1, ups1[...])
    for c in range(0, F, 128):
        cols = slice(c, c + 128)
        old = jnp.where(seen0 > 0.0, new0[:, cols], memory[:, cols].astype(F32))
        out[:, cols] = jnp.where(seen1 > 0.0, new1[:, cols], old).astype(BF)


def attend_kernel(pools, source, nearby, te, w_qkv, w_out, w_time, out):
    slots = pools.shape[0]
    events = source.shape[1]
    number = iota((slots, events), 0)
    for b in range(BATCHES):
        pool = pools[:, b * F : (b + 1) * F]
        kv = dot(pool, w_qkv[:, F:]).astype(BF)
        picked = dot_tn(hot(number == source[b : b + 1, :]), pool).astype(BF)
        query = dot(picked, w_qkv[:, :F]) * (1.0 / math.sqrt(HD))
        hits = [number == nearby[b, n : n + 1, :] for n in range(NBR)]
        near_te = [te[b, n].astype(F32) for n in range(NBR)]
        pieces = []
        for head in range(HEADS):
            cols = slice(head * HD, (head + 1) * HD)
            vcols = slice(F + head * HD, F + (head + 1) * HD)
            high, low = split(query[:, cols])
            by_slot = dot_nt(kv[:, cols], high) + dot_nt(kv[:, cols], low)
            by_time = dot_nt(w_time[:, cols], high) + dot_nt(w_time[:, cols], low)
            scores = [
                jnp.sum(
                    jnp.where(hits[n], by_slot, 0.0) + by_time * near_te[n],
                    axis=0,
                    keepdims=True,
                )
                for n in range(NBR)
            ]
            top = functools.reduce(jnp.maximum, scores)
            grown = [jnp.exp(s - top) for s in scores]
            scale = 1.0 / functools.reduce(jnp.add, grown)
            on_slot = jnp.zeros((slots, events), F32)
            on_time = jnp.zeros((TE, events), F32)
            for n in range(NBR):
                weight = grown[n] * scale
                on_slot = on_slot + jnp.where(hits[n], weight, 0.0)
                on_time = on_time + near_te[n] * weight
            s_high, s_low = split(on_slot)
            t_high, t_low = split(on_time)
            pieces.append(
                dot_tn(s_high, kv[:, vcols])
                + dot_tn(s_low, kv[:, vcols])
                + dot_tn(t_high, w_time[:, vcols])
                + dot_tn(t_low, w_time[:, vcols])
            )
        mixed = jnp.concatenate(pieces, axis=1).astype(BF)
        out[b] = dot(mixed, w_out[...]).astype(BF)


def call(kernel, n_in, outs, flops, args, name, **more):
    many = isinstance(outs, (list, tuple))
    moved = sum(a.size * a.dtype.itemsize for a in args)
    return pl.pallas_call(
        kernel,
        out_shape=outs,
        in_specs=more.pop("in_specs", [VSPEC] * n_in),
        out_specs=more.pop("out_specs", [VSPEC] * len(outs) if many else VSPEC),
        compiler_params=PARAMS,
        cost_estimate=pl.CostEstimate(flops=flops, bytes_accessed=moved, transcendentals=0),
        name=name,
        **more,
    )(*args)


def shape(dims, kind):
    return jax.ShapeDtypeStruct(dims, kind)


def body(
    memory,
    messages,
    slot_rows,
    counts,
    src_slot,
    nbr_slots,
    time_gap,
    time_freq,
    time_phase,
    gru_input,
    gru_hidden,
    gru_bias,
    attn_qkv,
    attn_out,
    time_proj,
):
    rows = memory.shape[0]
    slots = slot_rows.shape[2]
    events = src_slot.shape[1]
    section = lax.axis_index("section")
    core = lax.axis_index("shard") % 2
    sections = lax.axis_size("section")
    shards = lax.axis_size("shard")

    times = time_proj.reshape(32, 4, 256).transpose(1, 0, 2).reshape(128, 256)
    first = jnp.concatenate([gru_input, attn_qkv[:, :1152]], axis=1)
    second = jnp.concatenate([gru_hidden, attn_qkv[:, 1152:], attn_out, times], axis=1)
    half = jnp.where(core == 0, first, second)
    parts = [half] + [
        lax.ppermute(half, "section", [(i, (i + k) % sections) for i in range(sections)])
        for k in range(1, sections)
    ]
    mine = jnp.stack(parts)
    other = lax.ppermute(mine, "shard", [(i, i ^ 1) for i in range(shards)])

    alive = section < counts[:, 0]
    wanted = jnp.where(alive, slot_rows[:, 0, :, 0], rows)
    digits = jnp.stack(
        [wanted[0] // DIGIT, wanted[0] % DIGIT, wanted[1] // DIGIT, wanted[1] % DIGIT], axis=1
    ).astype(BF)
    sent = jnp.concatenate(
        [
            messages[0, 0, :, 0],
            messages[1, 0, :, 0],
            digits,
            jnp.zeros((slots, 128 - 4), BF),
        ],
        axis=1,
    )
    recv = lax.all_to_all(sent, "shard", split_axis=0, concat_axis=0, tiled=True)

    te = call(
        encode_kernel,
        3,
        shape((BATCHES, NBR, TE, events), BF),
        10**7,
        (time_gap.transpose(0, 2, 1), time_freq.reshape(TE, 1), time_phase.reshape(TE, 1)),
        "encode",
    )
    pos = jnp.stack([core, section]).astype(jnp.int32)
    w_in, w_hid, w_qkv, w_out, w_time = call(
        place_kernel,
        3,
        [shape((F, G), BF), shape((F, G), BF), shape((F, G), BF), shape((F, F), BF), shape((TE, 2 * F), BF)],
        0,
        (pos, mine, other),
        "place",
        in_specs=[SSPEC, ASPEC, ASPEC],
        out_specs=[ASPEC] * 5,
        scratch_shapes=[pltpu.SemaphoreType.DMA((36,))],
    )

    up0, gx1, base = call(
        first_kernel,
        5,
        [shape((slots + EXTRA, F), BF), shape((slots, G), F32), shape((slots, F), BF)],
        10**9,
        (recv, memory, w_in, w_hid, gru_bias),
        "first_batch",
    )
    ups0 = lax.all_gather(up0, "section", axis=0, tiled=True)
    up1 = call(
        functools.partial(second_kernel, float(rows)),
        6,
        shape((slots, F), BF),
        3 * 10**8,
        (recv, ups0, gx1, base, w_hid, gru_bias),
        "second_batch",
    )
    pools = lax.all_to_all(
        jnp.concatenate([up0[:slots], up1], axis=1), "shard", split_axis=0, concat_axis=0, tiled=True
    )
    ups1 = lax.all_gather(up1, "section", axis=0, tiled=True)
    memory_out = call(
        store_kernel,
        3,
        shape((rows, F), BF),
        10**9,
        (memory, ups0, ups1),
        "store",
        grid=(4,),
        in_specs=[
            pl.BlockSpec((rows // 4, F), lambda i: (i, 0)),
            pl.BlockSpec(ups0.shape, lambda i: (0, 0)),
            pl.BlockSpec(ups1.shape, lambda i: (0, 0)),
        ],
        out_specs=pl.BlockSpec((rows // 4, F), lambda i: (i, 0)),
    )
    embeddings = call(
        attend_kernel,
        7,
        shape((BATCHES, events, F), BF),
        10**9,
        (pools, src_slot, nbr_slots.transpose(0, 2, 1), te, w_qkv, w_out, w_time),
        "attend",
    )
    return memory_out, embeddings


def solution(mesh):
    in_specs = (
        P("shard", None),
        P(None, "shard", None, "section", None),
        P(None, "shard", None, "section"),
        P(None, "shard", None),
        P(None, ("section", "shard")),
        P(None, ("section", "shard"), None),
        P(None, ("section", "shard"), None),
        P(),
        P(),
        P("section", None),
        P("section", None),
        P(),
        P("section", None),
        P("section", None),
        P("section", None),
    )
    out_specs = (P("shard", None), P(None, ("section", "shard"), None))
    return jax.shard_map(body, mesh=mesh, in_specs=in_specs, out_specs=out_specs, check_vma=False)
```

profile of v0, /device:TPU:1, one launch (start us, length us, event | category | flops | bytes accessed | tf_op | source)
XLA Modules:
  0.0 155.5 jit_solution(919612649984085720)
XLA Ops:
  0.7 1.1 slice_bitcast_fusion.3
  3.7 3.9 %collective-permute-start = (bf16[128,2688]{1,0:T(8,128)(2,1)S(1)}, bf16[128,2688]{1,0:T(8,128)(2,1)S(1)}, u32[]{:S(2)}, u32[]{:S(2)}) collective-permute-start(bf16[128,2688]{1,0:T(8,128)(2,1)S(1)} %maximum_select_fusion.1), channel_id=1, source_target_pairs={{0,128},{128,256},{256,384},{384,0},{1,129},{129,257},{257,385},{3... | collective-permute-start | bytes 2064392 | tf_op jit(solution)/shard_map/ppermute | solution.py:287
  7.7 4.4 %collective-permute-start.1 = (bf16[128,2688]{1,0:T(8,128)(2,1)S(1)}, bf16[128,2688]{1,0:T(8,128)(2,1)S(1)}, u32[]{:S(2)}, u32[]{:S(2)}) collective-permute-start(bf16[128,2688]{1,0:T(8,128)(2,1)S(1)} %maximum_select_fusion.1), channel_id=1, source_target_pairs={{0,256},{128,384},{256,0},{384,128},{1,257},{129,385},{257,1},{385... | collective-permute-start | bytes 2064392 | tf_op jit(solution)/shard_map/ppermute | solution.py:287
  12.0 3.1 %collective-permute-start.2 = (bf16[128,2688]{1,0:T(8,128)(2,1)S(1)}, bf16[128,2688]{1,0:T(8,128)(2,1)S(1)}, u32[]{:S(2)}, u32[]{:S(2)}) collective-permute-start(bf16[128,2688]{1,0:T(8,128)(2,1)S(1)} %maximum_select_fusion.1), channel_id=1, source_target_pairs={{0,384},{128,0},{256,128},{384,256},{1,385},{129,1},{257,129},{385... | collective-permute-start | bytes 2064392 | tf_op jit(solution)/shard_map/ppermute | solution.py:287
  15.3 2.9 %collective-permute-done = bf16[128,2688]{1,0:T(8,128)(2,1)S(1)} collective-permute-done((bf16[128,2688]{1,0:T(8,128)(2,1)S(1)}, bf16[128,2688]{1,0:T(8,128)(2,1)S(1)}, u32[]{:S(2)}, u32[]{:S(2)}) %collective-permute-start) | collective-permute-done | bytes 688160 | tf_op jit(solution)/shard_map/ppermute | solution.py:287
  18.2 21.5 %collective-permute-done.1 = bf16[128,2688]{1,0:T(8,128)(2,1)S(1)} collective-permute-done((bf16[128,2688]{1,0:T(8,128)(2,1)S(1)}, bf16[128,2688]{1,0:T(8,128)(2,1)S(1)}, u32[]{:S(2)}, u32[]{:S(2)}) %collective-permute-start.1) | collective-permute-done | bytes 688160 | tf_op jit(solution)/shard_map/ppermute | solution.py:287
  39.7 0.9 collective-permute-done.2
  41.1 3.9 %collective-permute-start.3 = (bf16[4,128,2688]{2,1,0:T(8,128)(2,1)S(1)}, bf16[4,128,2688]{2,1,0:T(8,128)(2,1)}, u32[]{:S(2)}, u32[]{:S(2)}) collective-permute-start(bf16[4,128,2688]{2,1,0:T(8,128)(2,1)S(1)} %pad_maximum_fusion.mine), channel_id=1, source_target_pairs={{0,1},{1,0},{2,3},{3,2},{4,5},{5,4},{6,7},{7,6},{8,9},{9,8},{10,11... | collective-permute-start | bytes 8257544 | tf_op jit(solution)/shard_map/ppermute | solution.py:291
  47.1 1.1 reshape.312
  48.2 19.8 %all-to-all-start = ((bf16[128,2,576]{2,1,0:T(2,128)(2,1)}), bf16[128,2,576]{2,1,0:T(2,128)(2,1)}, u32[]{:S(2)}, u32[]{:S(2)}) async-start(bf16[128,2,576]{2,1,0:T(2,128)(2,1)} %reshape.312), calls=%async_computation | async-start | bytes 655360 | tf_op jit(solution)/shard_map/all_to_all | solution.py:307
  68.0 25.0 %all-to-all-done = bf16[128,2,576]{2,1,0:T(2,128)(2,1)} async-done(((bf16[128,2,576]{2,1,0:T(2,128)(2,1)}), bf16[128,2,576]{2,1,0:T(2,128)(2,1)}, u32[]{:S(2)}, u32[]{:S(2)}) %all-to-all-start) | async-done | bytes 294944 | tf_op jit(solution)/shard_map/all_to_all | solution.py:307
  93.1 2.5 %reshape.313 = bf16[128,1,1152]{2,1,0:T(2,128)(2,1)S(1)} reshape(bf16[128,2,576]{2,1,0:T(2,128)(2,1)} %all-to-all-done) | data formatting | bytes 589824
  95.7 2.7 %place.1 = (bf16[512,1536]{1,0:T(8,128)(2,1)S(1)}, bf16[512,1536]{1,0:T(8,128)(2,1)S(1)}, bf16[512,1536]{1,0:T(8,128)(2,1)S(1)}, bf16[512,512]{1,0:T(8,128)(2,1)S(1)}, bf16[128,1024]{1,0:T(8,128)(2,1)S(1)}) custom-call(s32[2]{0:T(128)S(1)} %pad_add_fusion.pos, bf16[4,128,2688]{2,1,0:T(8,128)(2,1)S(1)} %pad_maximum_fusion.mine, ...), custom_call_target="tpu_custom_call" | custom-call | bytes 5505032 | tf_op jit(solution)/shard_map/place/pallas_call | solution.py:241
  98.3 1.2 copy-done.3
  99.5 1.2 first_batch.1
  100.8 11.0 %all_gather.6.ups.ups0 = bf16[576,512]{1,0:T(8,128)(2,1)S(1)} all-gather(bf16[144,512]{1,0:T(8,128)(2,1)S(1)} %get-tuple-element.12), channel_id=1, replica_groups=mesh['section'=4,'shard'=128] {'section'}, dimensions={0}, use_global_device_ids=true | all-gather | bytes 737280 | tf_op jit(solution)/shard_map/all_gather | solution.py:338
  114.2 11.1 %all-to-all-start.1 = ((bf16[128,2,512]{2,1,0:T(2,128)(2,1)}), bf16[128,2,512]{2,1,0:T(2,128)(2,1)}, u32[]{:S(2)}, u32[]{:S(2)}) async-start(bf16[128,2,512]{2,1,0:T(2,128)(2,1)} %reshape.314), calls=%async_computation.1 | async-start | bytes 524288 | tf_op jit(solution)/shard_map/all_to_all | solution.py:347
  125.6 1.2 encode.1.te
  126.8 11.3 %all_gather.7.ups1 = bf16[512,512]{1,0:T(8,128)(2,1)S(1)} all-gather(bf16[128,512]{1,0:T(8,128)(2,1)S(1)} %second_batch.1), channel_id=1, replica_groups=mesh['section'=4,'shard'=128] {'section'}, dimensions={0}, use_global_device_ids=true | all-gather | bytes 655360 | tf_op jit(solution)/shard_map/all_gather | solution.py:350
  138.1 3.1 %store.1 = bf16[1024,512]{1,0:T(8,128)(2,1)} custom-call(bf16[1024,512]{1,0:T(8,128)(2,1)S(1)} %copy-done.1, bf16[576,512]{1,0:T(8,128)(2,1)S(1)} %all_gather.6.ups.ups0, bf16[512,512]{1,0:T(8,128)(2,1)S(1)} %all_gather.7.ups1), custom_call_target="tpu_custom_call" | custom-call | flops 1000000000 | bytes 2162688 | tf_op jit(solution)/shard_map/store/pallas_call | solution.py:241
  141.2 6.4 %all-to-all-done.1 = bf16[128,2,512]{2,1,0:T(2,128)(2,1)} async-done(((bf16[128,2,512]{2,1,0:T(2,128)(2,1)}), bf16[128,2,512]{2,1,0:T(2,128)(2,1)}, u32[]{:S(2)}, u32[]{:S(2)}) %all-to-all-start.1) | async-done | bytes 262176 | tf_op jit(solution)/shard_map/all_to_all | solution.py:347
  147.6 2.8 %reshape.315 = bf16[128,1,1024]{2,1,0:T(2,128)(2,1)} reshape(bf16[128,2,512]{2,1,0:T(2,128)(2,1)} %all-to-all-done.1) | data formatting | bytes 524288
  150.4 1.1 copy.62
  151.5 4.0 %attend.1 = bf16[2,128,512]{2,1,0:T(8,128)(2,1)} custom-call(bf16[128,1024]{1,0:T(8,128)(2,1)S(1)} %bitcast.75, s32[2,128]{1,0:T(2,128)S(1)} %copy-done.5, s32[2,10,128]{2,1,0:T(8,128)S(1)} %bitcast.77, bf16[2,10,128,128]{3,2,1,0:T(8,128)(2,1)S(1)} %encode.1.te, bf16[512,1536]{1,0:T(8,128)(2,1)S(1)} %copy-done.4, ...), custom_call_target="tpu_custom_call" | custom-call | flops 1000000000 | bytes 3288064 | tf_op jit(solution)/shard_map/attend/pallas_call | solution.py:241
  (61 shorter events, 7.4 us)
Async XLA Ops:
  0.6 2.9 %copy-start.6 = (bf16[128,1536]{1,0:T(8,128)(2,1)S(1)}, bf16[128,1536]{1,0:T(8,128)(2,1)}, u32[]{:S(2)}) copy-start(bf16[128,1536]{1,0:T(8,128)(2,1)} %param.24) | copy-start | bytes 1179652
  0.6 2.9 %copy-start.7 = (bf16[128,1536]{1,0:T(8,128)(2,1)S(1)}, bf16[128,1536]{1,0:T(8,128)(2,1)}, u32[]{:S(2)}) copy-start(bf16[128,1536]{1,0:T(8,128)(2,1)} %param.25) | copy-start | bytes 1179652
  0.7 2.9 %copy-start.8 = (bf16[128,512]{1,0:T(8,128)(2,1)S(1)}, bf16[128,512]{1,0:T(8,128)(2,1)}, u32[]{:S(2)}) copy-start(bf16[128,512]{1,0:T(8,128)(2,1)} %param.28) | copy-start | bytes 393220
  3.7 14.4 %collective-permute-start = (bf16[128,2688]{1,0:T(8,128)(2,1)S(1)}, bf16[128,2688]{1,0:T(8,128)(2,1)S(1)}, u32[]{:S(2)}, u32[]{:S(2)}) collective-permute-start(bf16[128,2688]{1,0:T(8,128)(2,1)S(1)} %maximum_select_fusion.1), channel_id=1, source_target_pairs={{0,128},{128,256},{256,384},{384,0},{1,129},{129,257},{257,385},{3... | collective-permute-start | bytes 2064392 | tf_op jit(solution)/shard_map/ppermute | solution.py:287
  7.7 32.0 %collective-permute-start.1 = (bf16[128,2688]{1,0:T(8,128)(2,1)S(1)}, bf16[128,2688]{1,0:T(8,128)(2,1)S(1)}, u32[]{:S(2)}, u32[]{:S(2)}) collective-permute-start(bf16[128,2688]{1,0:T(8,128)(2,1)S(1)} %maximum_select_fusion.1), channel_id=1, source_target_pairs={{0,256},{128,384},{256,0},{384,128},{1,257},{129,385},{257,1},{385... | collective-permute-start | bytes 2064392 | tf_op jit(solution)/shard_map/ppermute | solution.py:287
  12.0 28.6 %collective-permute-start.2 = (bf16[128,2688]{1,0:T(8,128)(2,1)S(1)}, bf16[128,2688]{1,0:T(8,128)(2,1)S(1)}, u32[]{:S(2)}, u32[]{:S(2)}) collective-permute-start(bf16[128,2688]{1,0:T(8,128)(2,1)S(1)} %maximum_select_fusion.1), channel_id=1, source_target_pairs={{0,384},{128,0},{256,128},{384,256},{1,385},{129,1},{257,129},{385... | collective-permute-start | bytes 2064392 | tf_op jit(solution)/shard_map/ppermute | solution.py:287
  40.6 4.3 %copy-start.13 = (s32[2,1,128]{2,1,0:T(1,128)S(1)}, s32[2,1,128]{2,1,0:T(1,128)}, u32[]{:S(2)}) copy-start(s32[2,1,128]{2,1,0:T(1,128)} %param.18) | copy-start | bytes 3076
  40.6 4.4 %copy-start.12 = (s32[2,1,128,1]{2,3,1,0:T(1,128)S(1)}, s32[2,1,128,1]{2,3,1,0:T(1,128)}, u32[]{:S(2)}) copy-start(s32[2,1,128,1]{2,3,1,0:T(1,128)} %param.17) | copy-start | bytes 3076
  40.6 5.0 %copy-start.9 = (bf16[2,1,128,1,512]{4,2,3,1,0:T(8,128)(2,1)S(1)}, bf16[2,1,128,1,512]{4,2,3,1,0:T(8,128)(2,1)}, u32[]{:S(2)}) copy-start(bf16[2,1,128,1,512]{4,2,3,1,0:T(8,128)(2,1)} %param.16) | copy-start | bytes 786436
  41.1 54.6 %collective-permute-start.3 = (bf16[4,128,2688]{2,1,0:T(8,128)(2,1)S(1)}, bf16[4,128,2688]{2,1,0:T(8,128)(2,1)}, u32[]{:S(2)}, u32[]{:S(2)}) collective-permute-start(bf16[4,128,2688]{2,1,0:T(8,128)(2,1)S(1)} %pad_maximum_fusion.mine), channel_id=1, source_target_pairs={{0,1},{1,0},{2,3},{3,2},{4,5},{5,4},{6,7},{7,6},{8,9},{9,8},{10,11... | collective-permute-start | bytes 8257544 | tf_op jit(solution)/shard_map/ppermute | solution.py:291
  48.2 44.9 %all-to-all-start = ((bf16[128,2,576]{2,1,0:T(2,128)(2,1)}), bf16[128,2,576]{2,1,0:T(2,128)(2,1)}, u32[]{:S(2)}, u32[]{:S(2)}) async-start(bf16[128,2,576]{2,1,0:T(2,128)(2,1)} %reshape.312), calls=%async_computation | async-start | bytes 655360 | tf_op jit(solution)/shard_map/all_to_all | solution.py:307
  95.6 3.9 %copy-start = (bf16[1024,512]{1,0:T(8,128)(2,1)S(1)}, bf16[1024,512]{1,0:T(8,128)(2,1)}, u32[]{:S(2)}) copy-start(bf16[1024,512]{1,0:T(8,128)(2,1)} %memory.3) | copy-start | bytes 3145732
  95.6 3.9 %copy-start.2 = (f32[2,1536]{1,0:T(2,128)S(1)}, f32[2,1536]{1,0:T(2,128)}, u32[]{:S(2)}) copy-start(f32[2,1536]{1,0:T(2,128)} %bias.3) | copy-start | bytes 36868
  98.3 1.2 copy-start.3
  112.5 12.9 %copy-start.14 = (f32[128]{0:T(128)S(1)}, f32[128]{0:T(128)}, u32[]{:S(2)}) copy-start(f32[128]{0:T(128)} %param.22) | copy-start | bytes 1540
  112.5 13.0 %copy-start.15 = (f32[128]{0:T(128)S(1)}, f32[128]{0:T(128)}, u32[]{:S(2)}) copy-start(f32[128]{0:T(128)} %param.23) | copy-start | bytes 1540
  112.5 13.1 %copy-start.10 = (f32[2,128,10]{1,0,2:T(2,128)S(1)}, f32[2,128,10]{1,0,2:T(2,128)}, u32[]{:S(2)}) copy-start(f32[2,128,10]{1,0,2:T(2,128)} %param.21) | copy-start | bytes 30724
  112.5 13.1 %copy-start.11 = (s32[2,128,10]{1,0,2:T(2,128)S(1)}, s32[2,128,10]{1,0,2:T(2,128)}, u32[]{:S(2)}) copy-start(s32[2,128,10]{1,0,2:T(2,128)} %param.20) | copy-start | bytes 30724
  113.3 24.8 %copy-start.1 = (bf16[1024,512]{1,0:T(8,128)(2,1)S(1)}, bf16[1024,512]{1,0:T(8,128)(2,1)}, u32[]{:S(2)}) copy-start(bf16[1024,512]{1,0:T(8,128)(2,1)} %memory.3) | copy-start | bytes 3145732
  114.2 33.4 %all-to-all-start.1 = ((bf16[128,2,512]{2,1,0:T(2,128)(2,1)}), bf16[128,2,512]{2,1,0:T(2,128)(2,1)}, u32[]{:S(2)}, u32[]{:S(2)}) async-start(bf16[128,2,512]{2,1,0:T(2,128)(2,1)} %reshape.314), calls=%async_computation.1 | async-start | bytes 524288 | tf_op jit(solution)/shard_map/all_to_all | solution.py:347
  141.2 10.3 %copy-start.4 = (bf16[512,1536]{1,0:T(8,128)(2,1)S(1)}, bf16[512,1536]{1,0:T(8,128)(2,1)}, u32[]{:S(2)}) copy-start(bf16[512,1536]{1,0:T(8,128)(2,1)} %copy-done.3) | copy-start | bytes 4718596
  141.2 10.3 %copy-start.5 = (s32[2,128]{1,0:T(2,128)S(1)}, s32[2,128]{1,0:T(2,128)}, u32[]{:S(2)}) copy-start(s32[2,128]{1,0:T(2,128)} %source.1) | copy-start | bytes 3076
where the time goes:
time: 156 us
  waiting for transfers between devices  56.8 us (36%)
  starting transfers between devices  46.1 us (30%)
  blocking collectives  22.3 us (14%)
  local copies, waits for them, and re-layouts  14 us (9%)
  Pallas kernels  12.9 us (8%)
  other arithmetic  2.43 us (2%)
    ppermute x3, waiting for transfers between devices, body(): lax.ppermute(half, 'section', [(i, (i + k) % sections) for i in range(sec...  25.3 us
    all_to_all x1, waiting for transfers between devices, body(): lax.all_to_all(sent, 'shard', split_axis=0, concat_axis=0, tiled=True)  25 us
    all_to_all x1, starting transfers between devices, body(): lax.all_to_all(sent, 'shard', split_axis=0, concat_axis=0, tiled=True)  19.8 us
    pallas_call x6, Pallas kernels, call(): pl.pallas_call(kernel, out_shape=outs, in_specs=more.pop('in_specs', [VSP...  12.9 us
    ppermute x3, starting transfers between devices, body(): lax.ppermute(half, 'section', [(i, (i + k) % sections) for i in range(sec...  11.4 us
    all_gather x1, blocking collectives, body(): ups1 = lax.all_gather(up1, 'section', axis=0, tiled=True)  11.3 us
    all_to_all x1, starting transfers between devices, body(): lax.all_to_all(jnp.concatenate([up0[:slots], up1], axis=1), 'shard', spli...  11.1 us
    all_gather x1, blocking collectives, body(): ups0 = lax.all_gather(up0, 'section', axis=0, tiled=True)  11 us
  transfers between devices with their start and end apart: 6, of which 5 were waited for; matrix products, arithmetic and copies ran while one was open for 4% of the time, Pallas kernels for 3%

commit v1 on v0

v1 whole, which is shorter than its diff:
```python
import functools
import math

import jax
import jax.numpy as jnp
from jax import lax
from jax.experimental import pallas as pl
from jax.experimental.pallas import tpu as pltpu
from jax.sharding import Mesh
from jax.sharding import PartitionSpec as P

HEADS = 2
HD = 256
BATCHES = 2
NBR = 10
F = 512
TE = 128
G = 3 * F
DIGIT = 32
EXTRA = 16
SHARD = ("chip", "core")
ALL = ("section", "chip", "core")
BF = jnp.bfloat16
F32 = jnp.float32
VMEM_LIMIT = 40 * 2**20
WIDE = 2 * G + G + F + 256
PACK_LIMIT = 56 * 2**20

SECTIONS = 4
HSPEC = pl.BlockSpec(memory_space=pltpu.HBM)
VSPEC = pl.BlockSpec(memory_space=pltpu.VMEM)


def dot(a, b):
    return jnp.dot(a, b, preferred_element_type=F32)


def dot_nt(a, b):
    return lax.dot_general(a, b, (((1,), (1,)), ((), ())), preferred_element_type=F32)


def dot_tn(a, b):
    return lax.dot_general(a, b, (((0,), (0,)), ((), ())), preferred_element_type=F32)


def split(x):
    high = x.astype(BF)
    return high, (x - high.astype(F32)).astype(BF)


def iota(shape, dim):
    return lax.broadcasted_iota(jnp.int32, shape, dim)


def hot(mask):
    return jnp.where(mask, 1.0, 0.0).astype(BF)


TWO_PI_HIGH = 6.28125
TWO_PI_LOW = 2.0 * math.pi - TWO_PI_HIGH
SERIES = [(-1.0) ** k / math.factorial(2 * k) for k in range(9)]


def cosine(x):
    turns = jnp.round(x * (1.0 / (2.0 * math.pi)))
    r = (x - turns * TWO_PI_HIGH) - turns * TWO_PI_LOW
    s = r * r
    y = jnp.full_like(s, SERIES[8])
    for k in range(7, -1, -1):
        y = y * s + SERIES[k]
    return y


def encode(gap, freq, phase, te):
    events = gap.shape[2]
    speed = jnp.broadcast_to(freq[...], (events, TE)).T
    start = jnp.broadcast_to(phase[...], (events, TE)).T
    for b in range(BATCHES):
        for n in range(NBR):
            te[b, n] = cosine(speed * gap[b, n : n + 1, :] + start).astype(BF)


def pack_kernel(dead, counts, wanted, messages, w_in, w_hid, w_qkv, w_out, w_time, sent, bundle, sems):
    pairs = []
    for array, at, width in [(w_in, 0, G), (w_hid, G, G), (w_qkv, 2 * G, G), (w_out, 3 * G, F)]:
        pairs.append((array, bundle.at[:, pl.ds(at, width)]))
    rows = w_time.shape[0]
    for q in range(4):
        piece = w_time.at[:, pl.ds(256 * q, 256)]
        pairs.append((piece, bundle.at[pl.ds(rows * q, rows), pl.ds(3 * G + F, 256)]))
    started = []
    for i, (source, target) in enumerate(pairs):
        copy = pltpu.make_async_copy(source, target, sems.at[i])
        copy.start()
        started.append(copy)
    number = jnp.where(counts[...] > lax.axis_index("section"), wanted[...], dead)
    high = (number // DIGIT).astype(F32)
    low = (number % DIGIT).astype(F32)
    lines = [high[0:1], low[0:1], high[1:2], low[1:2], jnp.zeros((124, number.shape[1]), F32)]
    digits = jnp.concatenate(lines, axis=0).T.astype(BF)
    for b in range(BATCHES):
        sent[:, b, :F] = messages[b]
        sent[:, b, F:] = digits
    wait(started)


def copies(pieces, col, width, target, sems):
    own, beside, across, far, far_across = pieces
    core, section = lax.axis_index("core"), lax.axis_index("section")
    count, half = own.shape[0], far.shape[0]
    turn = 1 - 2 * core
    started = []

    def put(source, step, first, length):
        where = (section + step + SECTIONS) % SECTIONS
        rows = pl.ds(pl.multiple_of(where * count + first, half), length)
        copy = pltpu.make_async_copy(source.at[:, pl.ds(col, width)], target.at[rows, :], sems.at[len(started)])
        copy.start()
        started.append(copy)

    put(own, 0, 0, count)
    put(beside, turn, 0, count)
    put(across, -turn, 0, count)
    put(far, 2, core * half, half)
    put(far_across, 2, half - core * half, half)
    return started


def wait(started):
    for copy in started:
        copy.wait()


def gates(gx, gh, h):
    reset = jax.nn.sigmoid(gx[:, :F] + gh[:, :F])
    update = jax.nn.sigmoid(gx[:, F : 2 * F] + gh[:, F : 2 * F])
    fresh = jnp.tanh(gx[:, 2 * F :] + reset * gh[:, 2 * F :])
    return ((1.0 - update) * fresh + update * h.astype(F32)).astype(BF)


def fetch_kernel(recv, memory, got, tail):
    slots = recv.shape[0]
    rows = memory.shape[0]
    digits = recv[:, 0, F:].astype(F32)
    tail[...] = jnp.zeros((EXTRA, F), BF)
    tail[:, :slots] = digits.T[:EXTRA, :].astype(BF)
    number = iota((slots, rows), 1).astype(F32)
    hot0 = hot(number == digits[:, 0:1] * DIGIT + digits[:, 1:2])
    hot1 = hot(number == digits[:, 2:3] * DIGIT + digits[:, 3:4])
    got[...] = dot(jnp.concatenate([hot0, hot1], axis=0), memory[...]).astype(BF)


def first_kernel(recv, got, tail, bias, *rest):
    pieces, (up, gx1, w_hid, w_in, sems) = rest[:5], rest[5:]
    in_copies = copies(pieces, 0, G, w_in, sems.at[0])
    hid_copies = copies(pieces, G, G, w_hid, sems.at[1])
    slots = recv.shape[0]
    up[slots:, :] = tail[...]
    sent = jnp.concatenate([recv[:, b, :F] for b in range(BATCHES)], axis=0)
    wait(in_copies)
    gx = dot(sent, w_in[...]) + bias[0:1, :]
    gx1[...] = gx[slots:]
    h = got[:slots, :]
    wait(hid_copies)
    gh = dot(h, w_hid[...]) + bias[1:2, :]
    up[:slots, :] = gates(gx[:slots], gh, h)


def numbers(ups, batch, slots):
    parts = []
    for t in range(ups.shape[0] // (slots + EXTRA)):
        at = t * (slots + EXTRA) + slots
        pair = ups[at : at + EXTRA, :slots].astype(F32)
        parts.append(pair[2 * batch : 2 * batch + 1] * DIGIT + pair[2 * batch + 1 : 2 * batch + 2])
    return jnp.concatenate(parts, axis=1)


def values(ups, slots):
    parts = []
    for t in range(ups.shape[0] // (slots + EXTRA)):
        at = t * (slots + EXTRA)
        parts.append(ups[at : at + slots, :])
    return jnp.concatenate(parts, axis=0)


def second_kernel(dead, recv, got, ups, gx1, up0, w_hid, bias, up, both):
    slots = recv.shape[0]
    digits = recv[:, 0, F:].astype(F32)
    mine = digits[:, 2:3] * DIGIT + digits[:, 3:4]
    same = (numbers(ups, 0, slots) == mine) & (mine < dead)
    any_same = jnp.max(jnp.where(same, 1.0, 0.0), axis=1, keepdims=True)
    moved = dot(hot(same), values(ups, slots))
    h = jnp.where(any_same > 0.0, moved, got[slots:, :].astype(F32)).astype(BF)
    gh = dot(h, w_hid[...]) + bias[1:2, :]
    new = gates(gx1[...], gh, h)
    up[...] = new
    both[:, 0, :] = up0[:slots, :]
    both[:, 1, :] = new


def store_kernel(memory, ups0, ups1, out):
    block = memory.shape[0]
    slots = ups0.shape[0] // SECTIONS - EXTRA
    number = (iota((block, 1), 0) + pl.program_id(0) * block).astype(F32)
    hot0 = hot(numbers(ups0, 0, slots) == number)
    hot1 = hot(numbers(ups0, 1, slots) == number)
    ones = jnp.ones((hot0.shape[1], 128), BF)
    seen0, seen1 = dot(hot0, ones), dot(hot1, ones)
    new0 = dot(hot0, values(ups0, slots))
    new1 = dot(hot1, ups1[...])
    for c in range(0, F, 128):
        cols = slice(c, c + 128)
        old = jnp.where(seen0 > 0.0, new0[:, cols], memory[:, cols].astype(F32))
        out[:, cols] = jnp.where(seen1 > 0.0, new1[:, cols], old).astype(BF)


def attend_kernel(pools, source, nearby, gap, freq, phase, *rest):
    pieces, (out, w, bundle_time, te, sems) = rest[:5], rest[5:]
    started = copies(pieces, 2 * G, G + F, w, sems.at[0])
    started += copies(pieces, 3 * G + F, 256, bundle_time, sems.at[1])
    slots = pools.shape[0]
    events = source.shape[1]
    number = iota((slots, events), 0)
    encode(gap, freq, phase, te)
    wait(started)
    quarter = w.shape[0] // SECTIONS
    w_time = [
        jnp.concatenate([bundle_time[t * quarter + 32 * q : t * quarter + 32 * q + 32, :] for t in range(SECTIONS)], axis=0)
        for q in range(2 * HEADS)
    ]
    for b in range(BATCHES):
        pool = pools[:, b, :]
        kv = dot(pool, w[:, F:G]).astype(BF)
        picked = dot_tn(hot(number == source[b : b + 1, :]), pool).astype(BF)
        query = dot(picked, w[:, :F]) * (1.0 / math.sqrt(HD))
        hits = [number == nearby[b, n : n + 1, :] for n in range(NBR)]
        near_te = [te[b, n].astype(F32) for n in range(NBR)]
        pieces = []
        for head in range(HEADS):
            cols = slice(head * HD, (head + 1) * HD)
            vcols = slice(F + head * HD, F + (head + 1) * HD)
            high, low = split(query[:, cols])
            by_slot = dot_nt(kv[:, cols], high) + dot_nt(kv[:, cols], low)
            by_time = dot_nt(w_time[head], high) + dot_nt(w_time[head], low)
            scores = [
                jnp.sum(
                    jnp.where(hits[n], by_slot, 0.0) + by_time * near_te[n],
                    axis=0,
                    keepdims=True,
                )
                for n in range(NBR)
            ]
            top = functools.reduce(jnp.maximum, scores)
            grown = [jnp.exp(s - top) for s in scores]
            scale = 1.0 / functools.reduce(jnp.add, grown)
            on_slot = jnp.zeros((slots, events), F32)
            on_time = jnp.zeros((TE, events), F32)
            for n in range(NBR):
                weight = grown[n] * scale
                on_slot = on_slot + jnp.where(hits[n], weight, 0.0)
                on_time = on_time + near_te[n] * weight
            s_high, s_low = split(on_slot)
            t_high, t_low = split(on_time)
            pieces.append(
                dot_tn(s_high, kv[:, vcols])
                + dot_tn(s_low, kv[:, vcols])
                + dot_tn(t_high, w_time[HEADS + head])
                + dot_tn(t_low, w_time[HEADS + head])
            )
        mixed = jnp.concatenate(pieces, axis=1).astype(BF)
        out[b] = dot(mixed, w[:, G:]).astype(BF)


def call(kernel, n_in, outs, flops, args, name, **more):
    many = isinstance(outs, (list, tuple))
    moved = sum(a.size * a.dtype.itemsize for a in args)
    return pl.pallas_call(
        kernel,
        out_shape=outs,
        in_specs=more.pop("in_specs", [VSPEC] * n_in),
        out_specs=more.pop("out_specs", [VSPEC] * len(outs) if many else VSPEC),
        compiler_params=pltpu.CompilerParams(vmem_limit_bytes=more.pop("limit", VMEM_LIMIT)),
        cost_estimate=pl.CostEstimate(flops=flops, bytes_accessed=moved, transcendentals=0),
        name=name,
        **more,
    )(*args)


def shape(dims, kind):
    return jax.ShapeDtypeStruct(dims, kind)


def body(
    memory,
    messages,
    slot_rows,
    counts,
    src_slot,
    nbr_slots,
    time_gap,
    time_freq,
    time_phase,
    gru_input,
    gru_hidden,
    gru_bias,
    attn_qkv,
    attn_out,
    time_proj,
):
    rows = memory.shape[0]
    slots = slot_rows.shape[2]
    events = src_slot.shape[1]
    core = lax.axis_index("core")

    sent, bundle = call(
        functools.partial(pack_kernel, rows),
        8,
        [
            shape((slots, BATCHES, F + 128), BF),
            shape((gru_input.shape[0], WIDE), BF),
        ],
        0,
        (
            counts[:, 0],
            slot_rows.reshape(BATCHES, slots),
            messages.reshape(BATCHES, slots, F),
            gru_input,
            gru_hidden,
            attn_qkv,
            attn_out,
            time_proj,
        ),
        "pack",
        in_specs=[VSPEC] * 3 + [HSPEC] * 5,
        out_specs=[VSPEC] * 2,
        scratch_shapes=[pltpu.SemaphoreType.DMA((8,))],
        limit=PACK_LIMIT,
    )
    near_pairs = []
    for t in range(SECTIONS):
        near_pairs.append(((t + 1) % SECTIONS * 2, t * 2))
        near_pairs.append(((t + 3) % SECTIONS * 2 + 1, t * 2 + 1))
    beside = lax.ppermute(bundle, ("section", "core"), near_pairs)
    count = gru_input.shape[0] // 2
    far = lax.ppermute(lax.dynamic_slice_in_dim(beside, core * count, count, 0), ("section", "core"), near_pairs)
    recv = lax.all_to_all(sent, SHARD, split_axis=0, concat_axis=0, tiled=True)
    swap = [(0, 1), (1, 0)]
    across = lax.ppermute(beside, "core", swap)
    recv, beside, far, across = lax.optimization_barrier((recv, beside, far, across))
    far_across = lax.ppermute(far, "core", swap)
    pieces = (bundle, beside, across, far, far_across)
    got, tail = call(
        fetch_kernel,
        2,
        [shape((2 * slots, F), BF), shape((EXTRA, F), BF)],
        3 * 10**8,
        (recv, memory),
        "fetch",
    )
    up0, gx1, w_hid = call(
        first_kernel,
        9,
        [shape((slots + EXTRA, F), BF), shape((slots, G), F32), shape((F, G), BF)],
        10**9,
        (recv, got, tail, gru_bias) + pieces,
        "first_batch",
        in_specs=[VSPEC] * 4 + [HSPEC] * 5,
        scratch_shapes=[pltpu.VMEM((F, G), BF), pltpu.SemaphoreType.DMA((2, 5))],
    )
    ups0 = lax.all_gather(up0, "section", axis=0, tiled=True)
    up1, both = call(
        functools.partial(second_kernel, float(rows)),
        7,
        [shape((slots, F), BF), shape((slots, BATCHES, F), BF)],
        3 * 10**8,
        (recv, got, ups0, gx1, up0, w_hid, gru_bias),
        "second_batch",
    )
    pools = lax.all_to_all(both, SHARD, split_axis=0, concat_axis=0, tiled=True)
    ups1 = lax.all_gather(up1, "section", axis=0, tiled=True)
    memory_out = call(
        store_kernel,
        3,
        shape((rows, F), BF),
        10**9,
        (memory, ups0, ups1),
        "store",
        grid=(4,),
        in_specs=[
            pl.BlockSpec((rows // 4, F), lambda i: (i, 0)),
            pl.BlockSpec(ups0.shape, lambda i: (0, 0)),
            pl.BlockSpec(ups1.shape, lambda i: (0, 0)),
        ],
        out_specs=pl.BlockSpec((rows // 4, F), lambda i: (i, 0)),
    )
    embeddings = call(
        attend_kernel,
        11,
        shape((BATCHES, events, F), BF),
        10**9,
        (
            pools,
            src_slot,
            nbr_slots.transpose(0, 2, 1),
            time_gap.transpose(0, 2, 1),
            time_freq.reshape(1, TE),
            time_phase.reshape(1, TE),
            *pieces,
        ),
        "attend",
        in_specs=[VSPEC] * 6 + [HSPEC] * 5,
        scratch_shapes=[
            pltpu.VMEM((F, G + F), BF),
            pltpu.VMEM((F, 256), BF),
            pltpu.VMEM((BATCHES, NBR, TE, events), BF),
            pltpu.SemaphoreType.DMA((2, 5)),
        ],
    )
    return memory_out, embeddings


def solution(mesh):
    sections, shards = mesh.devices.shape
    mesh = Mesh(mesh.devices.reshape(sections, shards // 2, 2), ALL)
    in_specs = (
        P(SHARD, None),
        P(None, SHARD, None, "section", None),
        P(None, SHARD, None, "section"),
        P(None, SHARD, None),
        P(None, ALL),
        P(None, ALL, None),
        P(None, ALL, None),
        P(),
        P(),
        P("section", None),
        P("section", None),
        P(),
        P("section", None),
        P("section", None),
        P("section", None),
    )
    out_specs = (P(SHARD, None), P(None, ALL, None))
    return jax.shard_map(body, mesh=mesh, in_specs=in_specs, out_specs=out_specs, check_vma=False)
```

time: 156 us -> 116 us (0.74)
  waiting for transfers between devices: 56.8 us -> 22.7 us
  local copies, waits for them, and re-layouts: 14 us -> 4.46 us
  Pallas kernels: 12.9 us -> 18.5 us
  other arithmetic: 2.43 us -> 0 us
    ppermute x4, waiting for transfers between devices: 25.3 us -> 0.01 us  [the longest x1 0.01 us: body(): beside = lax.ppermute(bundle, ('section', 'core'), near_pairs)]
    all_to_all x2, waiting for transfers between devices: 31.4 us -> 22.7 us  [the longest x1 18.6 us: body(): recv = lax.all_to_all(sent, SHARD, split_axis=0, concat_axis=0, tiled=True)]
    unnamed x40 -> x28, local copies, waits for them, and re-layouts: 9.63 us -> 3.56 us
    pallas_call x6, Pallas kernels: 12.9 us -> 18.5 us  [call(): pl.pallas_call(kernel, out_shape=outs, in_specs=more.pop('in_specs', [VSP...]
    concatenate x3 -> x0, local copies, waits for them, and re-layouts: 2.13 us -> none  [the longest x1 1.08 us: body(): first = jnp.concatenate([gru_input, attn_qkv[:, :1152]], axis=1)]
    ppermute x4, starting transfers between devices: 15.3 us -> 13.5 us  [the longest x1 3.95 us: body(): beside = lax.ppermute(bundle, ('section', 'core'), near_pairs)]
    all_to_all x3 -> x0, other arithmetic: 1.56 us -> none  [the longest x2 0.8 us: body(): lax.all_to_all(jnp.concatenate([up0[:slots], up1], axis=1), 'shard', spli...]
  transfers between devices with their start and end apart: 6 -> 6, of which waited for: 5 -> 2; matrix products, arithmetic and copies ran while one was open for 4% -> 1% of each run, Pallas kernels for 3% -> 3%
where the time goes in v1:
time: 116 us; the launch traced here: 114 us
  starting transfers between devices  44.7 us (39%)
  blocking collectives  23 us (20%)
  waiting for transfers between devices  22.7 us (20%)
  Pallas kernels  18.5 us (16%)
  local copies, waits for them, and re-layouts  4.46 us (4%)
    all_to_all x1, starting transfers between devices, body(): recv = lax.all_to_all(sent, SHARD, split_axis=0, concat_axis=0, tiled=True)  21.3 us
    all_to_all x1, waiting for transfers between devices, body(): recv = lax.all_to_all(sent, SHARD, split_axis=0, concat_axis=0, tiled=True)  18.6 us
    pallas_call x6, Pallas kernels, call(): pl.pallas_call(kernel, out_shape=outs, in_specs=more.pop('in_specs', [VSP...  18.5 us
    all_gather x1, blocking collectives, body(): ups1 = lax.all_gather(up1, 'section', axis=0, tiled=True)  12.6 us
    all_gather x1, blocking collectives, body(): ups0 = lax.all_gather(up0, 'section', axis=0, tiled=True)  10.5 us
    all_to_all x1, starting transfers between devices, body(): pools = lax.all_to_all(both, SHARD, split_axis=0, concat_axis=0, tiled=True)  9.93 us
    all_to_all x1, waiting for transfers between devices, body(): pools = lax.all_to_all(both, SHARD, split_axis=0, concat_axis=0, tiled=True)  4.11 us
    ppermute x1, starting transfers between devices, body(): beside = lax.ppermute(bundle, ('section', 'core'), near_pairs)  3.95 us
  transfers between devices with their start and end apart: 6, of which 2 were waited for; matrix products, arithmetic and copies ran while one was open for 1% of the time, Pallas kernels for 3%

profile of v1, /device:TPU:1, one launch (start us, length us, event | category | flops | bytes accessed | tf_op | source)
XLA Modules:
  0.0 114.4 jit_solution(12220318384092388428)
XLA Ops:
  0.6 3.5 %pack.1 = (bf16[128,2,640]{2,1,0:T(2,128)(2,1)}, bf16[128,5376]{1,0:T(8,128)(2,1)}) custom-call(s32[2,128]{1,0:T(2,128)} %bitcast.16, s32[2,128]{1,0:T(2,128)} %bitcast.17, bf16[2,128,512]{2,1,0:T(8,128)(2,1)} %bitcast.15, bf16[128,1536]{1,0:T(8,128)(2,1)} %w_in.1, bf16[128,1536]{1,0:T(8,128)(2,1)} %w_hid.1, bf16[128,1536]{1,0:T(8,128)(2,1)} %w_qkv.1, ...), custom_call_target="tpu_custom_call" | custom-call | bytes 1640448 | tf_op jit(solution)/shard_map/pack/pallas_call | solution.py:277
  4.2 3.9 %collective-permute-start = (bf16[128,5376]{1,0:T(8,128)(2,1)}, bf16[128,5376]{1,0:T(8,128)(2,1)S(1)}, u32[]{:S(2)}, u32[]{:S(2)}) collective-permute-start(bf16[128,5376]{1,0:T(8,128)(2,1)} %get-tuple-element.16.rest_0_), channel_id=1, source_target_pairs={{128,0},{385,1},{256,128},{1,129},{384,256},{129,257},{0,384},{257... | collective-permute-start | bytes 4128776 | tf_op jit(solution)/shard_map/ppermute | solution.py:343
  8.1 21.3 %all-to-all-start = ((bf16[128,2,640]{2,1,0:T(2,128)(2,1)}), bf16[128,2,640]{2,1,0:T(2,128)(2,1)S(1)}, u32[]{:S(2)}, u32[]{:S(2)}) async-start(bf16[128,2,640]{2,1,0:T(2,128)(2,1)} %get-tuple-element.15), calls=%async_computation | async-start | bytes 655360 | tf_op jit(solution)/shard_map/all_to_all | solution.py:346
  29.4 0.0 copy-start.7
  29.4 0.0 collective-permute-done.rest_1_
  29.4 3.9 %collective-permute-start.2 = (bf16[128,5376]{1,0:T(8,128)(2,1)S(1)}, bf16[128,5376]{1,0:T(8,128)(2,1)}, u32[]{:S(2)}, u32[]{:S(2)}) collective-permute-start(bf16[128,5376]{1,0:T(8,128)(2,1)S(1)} %collective-permute-done.rest_1_), channel_id=1, source_target_pairs={{0,1},{1,0},{2,3},{3,2},{4,5},{5,4},{6,7},{7,6},{8,9},{9,8},{10,11... | collective-permute-start | bytes 4128776 | tf_op jit(solution)/shard_map/ppermute | solution.py:348
  33.4 0.9 constant_dynamic-slice_fusion
  34.3 1.9 %collective-permute-start.1 = (bf16[64,5376]{1,0:T(8,128)(2,1)}, bf16[64,5376]{1,0:T(8,128)(2,1)}, u32[]{:S(2)}, u32[]{:S(2)}) collective-permute-start(bf16[64,5376]{1,0:T(8,128)(2,1)} %constant_dynamic-slice_fusion), channel_id=1, source_target_pairs={{128,0},{385,1},{256,128},{1,129},{384,256},{129,257},{0,384},{257... | collective-permute-start | bytes 2064392 | tf_op jit(solution)/shard_map/ppermute | solution.py:345
  36.2 18.6 %all-to-all-done.recv = bf16[128,2,640]{2,1,0:T(2,128)(2,1)S(1)} async-done(((bf16[128,2,640]{2,1,0:T(2,128)(2,1)}), bf16[128,2,640]{2,1,0:T(2,128)(2,1)S(1)}, u32[]{:S(2)}, u32[]{:S(2)}) %all-to-all-start) | async-done | bytes 327712 | tf_op jit(solution)/shard_map/all_to_all | solution.py:346
  54.8 3.7 %collective-permute-start.3 = (bf16[64,5376]{1,0:T(8,128)(2,1)}, bf16[64,5376]{1,0:T(8,128)(2,1)S(1)}, u32[]{:S(2)}, u32[]{:S(2)}) collective-permute-start(bf16[64,5376]{1,0:T(8,128)(2,1)} %collective-permute-done.1.rest_3_), channel_id=1, source_target_pairs={{0,1},{1,0},{2,3},{3,2},{4,5},{5,4},{6,7},{7,6},{8,9},{9,8},{10,11... | collective-permute-start | bytes 2064392 | tf_op jit(solution)/shard_map/ppermute | solution.py:350
  58.5 0.0 copy-start.5
  58.6 1.2 %copy-done.5 = bf16[1024,512]{1,0:T(8,128)(2,1)S(1)} copy-done((bf16[1024,512]{1,0:T(8,128)(2,1)S(1)}, bf16[1024,512]{1,0:T(8,128)(2,1)}, u32[]{:S(2)}) %copy-start.5) | copy-done | bytes 1048600
  59.8 0.9 fetch.1
  60.6 0.0 collective-permute-done.3.rest_4_
  60.7 2.4 %first_batch.1 = (bf16[144,512]{1,0:T(8,128)(2,1)S(1)}, f32[128,1536]{1,0:T(8,128)S(1)}, bf16[512,1536]{1,0:T(8,128)(2,1)S(1)}) custom-call(bf16[128,2,640]{2,1,0:T(2,128)(2,1)S(1)} %all-to-all-done.recv, bf16[256,512]{1,0:T(8,128)(2,1)S(1)} %get-tuple-element.18.got, bf16[16,512]{1,0:T(8,128)(2,1)S(1)} %get-tuple-element.19.tail, f32[2,1536]{1,0:T(2,128)S(1)} %copy-done.7, ...), custom_call_target="tpu_custom_call" | custom-call | flops 1000000000 | bytes 6123520 | tf_op jit(solution)/shard_map/first_batch/pallas_call | solution.py:277
  63.1 10.5 %all_gather.6.ups.ups0 = bf16[576,512]{1,0:T(8,128)(2,1)S(1)} all-gather(bf16[144,512]{1,0:T(8,128)(2,1)S(1)} %get-tuple-element.23.up0), channel_id=1, replica_groups=mesh['section'=4,'chip'=64,'core'=2] {'section'}, dimensions={0}, use_global_device_ids=true | all-gather | bytes 737280 | tf_op jit(solution)/shard_map/all_gather | solution.py:370
  73.6 1.8 %second_batch.1 = (bf16[128,512]{1,0:T(8,128)(2,1)S(1)}, bf16[128,2,512]{2,1,0:T(2,128)(2,1)}) custom-call(bf16[128,2,640]{2,1,0:T(2,128)(2,1)S(1)} %all-to-all-done.recv, bf16[256,512]{1,0:T(8,128)(2,1)S(1)} %get-tuple-element.18.got, bf16[576,512]{1,0:T(8,128)(2,1)S(1)} %all_gather.6.ups.ups0, f32[128,1536]{1,0:T(8,128)S(1)} %get-tuple-element.24.gx1, ...), custom_call_target="tpu_custom_call" | custom-call | flops 300000000 | bytes 3698688 | tf_op jit(solution)/shard_map/second_batch/pallas_call | solution.py:277
  75.3 9.9 %all-to-all-start.1 = ((bf16[128,2,512]{2,1,0:T(2,128)(2,1)}), bf16[128,2,512]{2,1,0:T(2,128)(2,1)}, u32[]{:S(2)}, u32[]{:S(2)}) async-start(bf16[128,2,512]{2,1,0:T(2,128)(2,1)} %get-tuple-element.27), calls=%async_computation.1 | async-start | bytes 524288 | tf_op jit(solution)/shard_map/all_to_all | solution.py:379
  85.3 12.6 %all_gather.7.ups1 = bf16[512,512]{1,0:T(8,128)(2,1)S(1)} all-gather(bf16[128,512]{1,0:T(8,128)(2,1)S(1)} %get-tuple-element.26), channel_id=1, replica_groups=mesh['section'=4,'chip'=64,'core'=2] {'section'}, dimensions={0}, use_global_device_ids=true | all-gather | bytes 655360 | tf_op jit(solution)/shard_map/all_gather | solution.py:380
  97.9 1.1 copy-done.4
  99.0 1.2 %copy-done.6 = bf16[1024,512]{1,0:T(8,128)(2,1)S(1)} copy-done((bf16[1024,512]{1,0:T(8,128)(2,1)S(1)}, bf16[1024,512]{1,0:T(8,128)(2,1)}, u32[]{:S(2)}) %copy-start.6) | copy-done | bytes 1048600
  100.2 3.1 %store.1 = bf16[1024,512]{1,0:T(8,128)(2,1)} custom-call(bf16[1024,512]{1,0:T(8,128)(2,1)S(1)} %copy-done.6, bf16[576,512]{1,0:T(8,128)(2,1)S(1)} %copy-done.4, bf16[512,512]{1,0:T(8,128)(2,1)S(1)} %all_gather.7.ups1), custom_call_target="tpu_custom_call" | custom-call | flops 1000000000 | bytes 2162688 | tf_op jit(solution)/shard_map/store/pallas_call | solution.py:277
  103.3 4.1 %all-to-all-done.1.pools = bf16[128,2,512]{2,1,0:T(2,128)(2,1)} async-done(((bf16[128,2,512]{2,1,0:T(2,128)(2,1)}), bf16[128,2,512]{2,1,0:T(2,128)(2,1)}, u32[]{:S(2)}, u32[]{:S(2)}) %all-to-all-start.1) | async-done | bytes 262176 | tf_op jit(solution)/shard_map/all_to_all | solution.py:379
  107.5 6.8 %attend.1 = bf16[2,128,512]{2,1,0:T(8,128)(2,1)} custom-call(bf16[128,2,512]{2,1,0:T(2,128)(2,1)} %all-to-all-done.1.pools, s32[2,128]{1,0:T(2,128)S(1)} %copy-done.8, s32[2,10,128]{2,1,0:T(8,128)S(1)} %bitcast.11, f32[2,10,128]{2,1,0:T(8,128)S(1)} %bitcast.12, f32[1,128]{1,0:T(1,128)S(1)} %bitcast.13, f32[1,128]{1,0:T(1,128)S(1)} %bitcast.14, ...), custom_call_target="tpu_custom_call" | custom-call | flops 1000000000 | bytes 5789696 | tf_op jit(solution)/shard_map/attend/pallas_call | solution.py:277
  (25 shorter events, 0.1 us)
Async XLA Ops:
  4.2 25.3 %collective-permute-start = (bf16[128,5376]{1,0:T(8,128)(2,1)}, bf16[128,5376]{1,0:T(8,128)(2,1)S(1)}, u32[]{:S(2)}, u32[]{:S(2)}) collective-permute-start(bf16[128,5376]{1,0:T(8,128)(2,1)} %get-tuple-element.16.rest_0_), channel_id=1, source_target_pairs={{128,0},{385,1},{256,128},{1,129},{384,256},{129,257},{0,384},{257... | collective-permute-start | bytes 4128776 | tf_op jit(solution)/shard_map/ppermute | solution.py:343
  8.1 46.7 %all-to-all-start = ((bf16[128,2,640]{2,1,0:T(2,128)(2,1)}), bf16[128,2,640]{2,1,0:T(2,128)(2,1)S(1)}, u32[]{:S(2)}, u32[]{:S(2)}) async-start(bf16[128,2,640]{2,1,0:T(2,128)(2,1)} %get-tuple-element.15), calls=%async_computation | async-start | bytes 655360 | tf_op jit(solution)/shard_map/all_to_all | solution.py:346
  29.4 31.3 %copy-start.7 = (f32[2,1536]{1,0:T(2,128)S(1)}, f32[2,1536]{1,0:T(2,128)}, u32[]{:S(2)}) copy-start(f32[2,1536]{1,0:T(2,128)} %bias.3) | copy-start | bytes 36868
  29.4 31.2 %copy-start = (bf16[128,5376]{1,0:T(8,128)(2,1)S(1)}, bf16[128,5376]{1,0:T(8,128)(2,1)}, u32[]{:S(2)}) copy-start(bf16[128,5376]{1,0:T(8,128)(2,1)} %get-tuple-element.16.rest_0_) | copy-start | bytes 4128772
  29.4 25.3 %collective-permute-start.2 = (bf16[128,5376]{1,0:T(8,128)(2,1)S(1)}, bf16[128,5376]{1,0:T(8,128)(2,1)}, u32[]{:S(2)}, u32[]{:S(2)}) collective-permute-start(bf16[128,5376]{1,0:T(8,128)(2,1)S(1)} %collective-permute-done.rest_1_), channel_id=1, source_target_pairs={{0,1},{1,0},{2,3},{3,2},{4,5},{5,4},{6,7},{7,6},{8,9},{9,8},{10,11... | collective-permute-start | bytes 4128776 | tf_op jit(solution)/shard_map/ppermute | solution.py:348
  34.3 20.5 %collective-permute-start.1 = (bf16[64,5376]{1,0:T(8,128)(2,1)}, bf16[64,5376]{1,0:T(8,128)(2,1)}, u32[]{:S(2)}, u32[]{:S(2)}) collective-permute-start(bf16[64,5376]{1,0:T(8,128)(2,1)} %constant_dynamic-slice_fusion), channel_id=1, source_target_pairs={{128,0},{385,1},{256,128},{1,129},{384,256},{129,257},{0,384},{257... | collective-permute-start | bytes 2064392 | tf_op jit(solution)/shard_map/ppermute | solution.py:345
  54.8 5.9 %collective-permute-start.3 = (bf16[64,5376]{1,0:T(8,128)(2,1)}, bf16[64,5376]{1,0:T(8,128)(2,1)S(1)}, u32[]{:S(2)}, u32[]{:S(2)}) collective-permute-start(bf16[64,5376]{1,0:T(8,128)(2,1)} %collective-permute-done.1.rest_3_), channel_id=1, source_target_pairs={{0,1},{1,0},{2,3},{3,2},{4,5},{5,4},{6,7},{7,6},{8,9},{9,8},{10,11... | collective-permute-start | bytes 2064392 | tf_op jit(solution)/shard_map/ppermute | solution.py:350
  58.5 1.2 %copy-start.5 = (bf16[1024,512]{1,0:T(8,128)(2,1)S(1)}, bf16[1024,512]{1,0:T(8,128)(2,1)}, u32[]{:S(2)}) copy-start(bf16[1024,512]{1,0:T(8,128)(2,1)} %memory.3) | copy-start | bytes 3145732
  60.7 2.4 %copy-start.1 = (bf16[64,5376]{1,0:T(8,128)(2,1)}, bf16[64,5376]{1,0:T(8,128)(2,1)S(1)}, u32[]{:S(2)}) copy-start(bf16[64,5376]{1,0:T(8,128)(2,1)S(1)} %collective-permute-done.3.rest_4_) | copy-start | bytes 2064388
  73.6 1.8 %copy-start.3 = (bf16[576,512]{1,0:T(8,128)(2,1)}, bf16[576,512]{1,0:T(8,128)(2,1)S(1)}, u32[]{:S(2)}) copy-start(bf16[576,512]{1,0:T(8,128)(2,1)S(1)} %all_gather.6.ups.ups0) | copy-start | bytes 1769476
  73.6 11.7 %copy-start.11 = (s32[2,128,10]{1,0,2:T(2,128)S(1)}, s32[2,128,10]{1,0,2:T(2,128)}, u32[]{:S(2)}) copy-start(s32[2,128,10]{1,0,2:T(2,128)} %param.20) | copy-start | bytes 30724
  73.6 11.8 %copy-start.12 = (f32[2,128,10]{1,0,2:T(2,128)S(1)}, f32[2,128,10]{1,0,2:T(2,128)}, u32[]{:S(2)}) copy-start(f32[2,128,10]{1,0,2:T(2,128)} %param.21) | copy-start | bytes 30724
  75.3 32.1 %all-to-all-start.1 = ((bf16[128,2,512]{2,1,0:T(2,128)(2,1)}), bf16[128,2,512]{2,1,0:T(2,128)(2,1)}, u32[]{:S(2)}, u32[]{:S(2)}) async-start(bf16[128,2,512]{2,1,0:T(2,128)(2,1)} %get-tuple-element.27), calls=%async_computation.1 | async-start | bytes 524288 | tf_op jit(solution)/shard_map/all_to_all | solution.py:379
  97.9 1.1 copy-start.4
  99.0 1.2 %copy-start.6 = (bf16[1024,512]{1,0:T(8,128)(2,1)S(1)}, bf16[1024,512]{1,0:T(8,128)(2,1)}, u32[]{:S(2)}) copy-start(bf16[1024,512]{1,0:T(8,128)(2,1)} %memory.3) | copy-start | bytes 3145732
  100.2 7.3 %copy-start.2 = (bf16[64,5376]{1,0:T(8,128)(2,1)S(1)}, bf16[64,5376]{1,0:T(8,128)(2,1)}, u32[]{:S(2)}) copy-start(bf16[64,5376]{1,0:T(8,128)(2,1)} %copy-done.1) | copy-start | bytes 2064388
  100.2 7.3 %copy-start.8 = (s32[2,128]{1,0:T(2,128)S(1)}, s32[2,128]{1,0:T(2,128)}, u32[]{:S(2)}) copy-start(s32[2,128]{1,0:T(2,128)} %source.1) | copy-start | bytes 3076
  100.2 7.3 %copy-start.9 = (f32[128]{0:T(128)S(1)}, f32[128]{0:T(128)}, u32[]{:S(2)}) copy-start(f32[128]{0:T(128)} %param.22) | copy-start | bytes 1540
  100.2 7.3 %copy-start.10 = (f32[128]{0:T(128)S(1)}, f32[128]{0:T(128)}, u32[]{:S(2)}) copy-start(f32[128]{0:T(128)} %param.23) | copy-start | bytes 1540

commit v2 on v1

--- a/solution.py
+++ b/solution.py
@@ -183,6 +183,11 @@
     return jnp.concatenate(parts, axis=0)
 
 
+def tile_order():
+    to, at = iota((128, 128), 0), iota((128, 128), 1)
+    return hot((at % 16) * 8 + at // 16 == to)
+
+
 def second_kernel(dead, recv, got, ups, gx1, up0, w_hid, bias, up, both):
     slots = recv.shape[0]
     digits = recv[:, 0, F:].astype(F32)
@@ -194,8 +199,12 @@
     gh = dot(h, w_hid[...]) + bias[1:2, :]
     new = gates(gx1[...], gh, h)
     up[...] = new
-    both[:, 0, :] = up0[:slots, :]
-    both[:, 1, :] = new
+    order = tile_order()
+    for i in range(slots // 16):
+        at = slice(16 * i, 16 * i + 16)
+        lines = [up0[at, 128 * c : 128 * c + 128] for c in range(4)]
+        lines += [new[at, 128 * c : 128 * c + 128] for c in range(4)]
+        both[128 * i : 128 * i + 128, :] = dot(order, jnp.concatenate(lines, axis=0)).astype(BF)
 
 
 def store_kernel(memory, ups0, ups1, out):
@@ -214,37 +223,48 @@
         out[:, cols] = jnp.where(seen1 > 0.0, new1[:, cols], old).astype(BF)
 
 
-def attend_kernel(pools, source, nearby, gap, freq, phase, *rest):
-    pieces, (out, w, bundle_time, te, sems) = rest[:5], rest[5:]
-    started = copies(pieces, 2 * G, G + F, w, sems.at[0])
-    started += copies(pieces, 3 * G + F, 256, bundle_time, sems.at[1])
-    slots = pools.shape[0]
+def place_kernel(*refs):
+    pieces, (w, w_late, sems) = refs[:5], refs[5:]
+    wait(copies(pieces, 2 * G, G, w, sems.at[0]) + copies(pieces, 3 * G, F + 256, w_late, sems.at[1]))
+
+
+def attend_kernel(pools, source, nearby, gap, freq, phase, w, w_late, out, te):
+    slots = pools.shape[0] // 8
     events = source.shape[1]
     number = iota((slots, events), 0)
+    order = tile_order()
+    lines = [[] for _ in range(BATCHES)]
+    for i in range(slots // 16):
+        block = dot_tn(order, pools[128 * i : 128 * i + 128, :]).astype(BF)
+        for b in range(BATCHES):
+            parts = [block[64 * b + 16 * c : 64 * b + 16 * c + 16] for c in range(4)]
+            lines[b].append(jnp.concatenate(parts, axis=1))
+    pool = [jnp.concatenate(lines[b], axis=0) for b in range(BATCHES)]
+    picked = [dot_tn(hot(number == source[b : b + 1, :]), pool[b]).astype(BF) for b in range(BATCHES)]
     encode(gap, freq, phase, te)
-    wait(started)
-    quarter = w.shape[0] // SECTIONS
+    kv = dot(jnp.concatenate(pool, axis=0), w[:, F:]).astype(BF)
+    query = dot(jnp.concatenate(picked, axis=0), w[:, :F]) * (1.0 / math.sqrt(HD))
+    quarter = w_late.shape[0] // SECTIONS
     w_time = [
-        jnp.concatenate([bundle_time[t * quarter + 32 * q : t * quarter + 32 * q + 32, :] for t in range(SECTIONS)], axis=0)
+        jnp.concatenate([w_late[t * quarter + 32 * q : t * quarter + 32 * q + 32, F:] for t in range(SECTIONS)], axis=0)
         for q in range(2 * HEADS)
     ]
+    mixed = []
     for b in range(BATCHES):
-        pool = pools[:, b, :]
-        kv = dot(pool, w[:, F:G]).astype(BF)
-        picked = dot_tn(hot(number == source[b : b + 1, :]), pool).astype(BF)
-        query = dot(picked, w[:, :F]) * (1.0 / math.sqrt(HD))
         hits = [number == nearby[b, n : n + 1, :] for n in range(NBR)]
-        near_te = [te[b, n].astype(F32) for n in range(NBR)]
-        pieces = []
+        pieces_of = []
         for head in range(HEADS):
             cols = slice(head * HD, (head + 1) * HD)
             vcols = slice(F + head * HD, F + (head + 1) * HD)
-            high, low = split(query[:, cols])
-            by_slot = dot_nt(kv[:, cols], high) + dot_nt(kv[:, cols], low)
-            by_time = dot_nt(w_time[head], high) + dot_nt(w_time[head], low)
+            own = slice(b * slots, (b + 1) * slots)
+            high, low = split(query[b * events : (b + 1) * events, cols])
+            keys = jnp.concatenate([kv[own, cols], w_time[head]], axis=0)
+            twice = dot_nt(keys, jnp.concatenate([high, low], axis=0))
+            product = twice[:, :events] + twice[:, events:]
+            by_slot, by_time = product[:slots], product[slots:]
             scores = [
                 jnp.sum(
-                    jnp.where(hits[n], by_slot, 0.0) + by_time * near_te[n],
+                    jnp.where(hits[n], by_slot, 0.0) + by_time * te[b, n].astype(F32),
                     axis=0,
                     keepdims=True,
                 )
@@ -258,17 +278,15 @@
             for n in range(NBR):
                 weight = grown[n] * scale
                 on_slot = on_slot + jnp.where(hits[n], weight, 0.0)
-                on_time = on_time + near_te[n] * weight
-            s_high, s_low = split(on_slot)
-            t_high, t_low = split(on_time)
-            pieces.append(
-                dot_tn(s_high, kv[:, vcols])
-                + dot_tn(s_low, kv[:, vcols])
-                + dot_tn(t_high, w_time[HEADS + head])
-                + dot_tn(t_low, w_time[HEADS + head])
-            )
-        mixed = jnp.concatenate(pieces, axis=1).astype(BF)
-        out[b] = dot(mixed, w[:, G:]).astype(BF)
+                on_time = on_time + te[b, n].astype(F32) * weight
+            w_high, w_low = split(jnp.concatenate([on_slot, on_time], axis=0))
+            found = jnp.concatenate([kv[own, vcols], w_time[HEADS + head]], axis=0)
+            twice = dot_tn(jnp.concatenate([w_high, w_low], axis=1), found)
+            pieces_of.append(twice[:events] + twice[events:])
+        mixed.append(jnp.concatenate(pieces_of, axis=1).astype(BF))
+    result = dot(jnp.concatenate(mixed, axis=0), w_late[:, :F]).astype(BF)
+    for b in range(BATCHES):
+        out[b] = result[b * events : (b + 1) * events]
 
 
 def call(kernel, n_in, outs, flops, args, name, **more):
@@ -371,7 +389,7 @@
     up1, both = call(
         functools.partial(second_kernel, float(rows)),
         7,
-        [shape((slots, F), BF), shape((slots, BATCHES, F), BF)],
+        [shape((slots, F), BF), shape((slots * 8, 128), BF)],
         3 * 10**8,
         (recv, got, ups0, gx1, up0, w_hid, gru_bias),
         "second_batch",
@@ -393,9 +411,19 @@
         ],
         out_specs=pl.BlockSpec((rows // 4, F), lambda i: (i, 0)),
     )
+    w, w_late = call(
+        place_kernel,
+        5,
+        [shape((F, G), BF), shape((F, F + 256), BF)],
+        0,
+        pieces,
+        "place",
+        in_specs=[HSPEC] * 5,
+        scratch_shapes=[pltpu.SemaphoreType.DMA((2, 5))],
+    )
     embeddings = call(
         attend_kernel,
-        11,
+        8,
         shape((BATCHES, events, F), BF),
         10**9,
         (
@@ -405,15 +433,12 @@
             time_gap.transpose(0, 2, 1),
             time_freq.reshape(1, TE),
             time_phase.reshape(1, TE),
-            *pieces,
+            w,
+            w_late,
         ),
         "attend",
-        in_specs=[VSPEC] * 6 + [HSPEC] * 5,
         scratch_shapes=[
-            pltpu.VMEM((F, G + F), BF),
-            pltpu.VMEM((F, 256), BF),
             pltpu.VMEM((BATCHES, NBR, TE, events), BF),
-            pltpu.SemaphoreType.DMA((2, 5)),
         ],
     )
     return memory_out, embeddings

time: 116 us -> 114 us (0.983)
  waiting for transfers between devices: 22.7 us -> 21 us
    all_to_all x1, waiting for transfers between devices: 4.11 us -> 2.36 us  [body(): pools = lax.all_to_all(both, SHARD, split_axis=0, concat_axis=0, tiled=True)]
    pallas_call x6 -> x7, Pallas kernels: 18.5 us -> 17.5 us  [call(): pl.pallas_call(kernel, out_shape=outs, in_specs=more.pop('in_specs', [VSP...]
    unnamed x28 -> x36, local copies, waits for them, and re-layouts: 3.56 us -> 4.44 us
  transfers between devices with their start and end apart: 6 -> 6, of which waited for: 2 -> 2; matrix products, arithmetic and copies ran while one was open for 1% -> 1% of each run, Pallas kernels for 3% -> 5%
where the time goes in v2:
time: 114 us; the launch traced here: 112 us
  starting transfers between devices  44.2 us (39%)
  blocking collectives  22.8 us (20%)
  waiting for transfers between devices  21 us (18%)
  Pallas kernels  17.5 us (15%)
  local copies, waits for them, and re-layouts  5.34 us (5%)
    all_to_all x1, starting transfers between devices, body(): recv = lax.all_to_all(sent, SHARD, split_axis=0, concat_axis=0, tiled=True)  21.3 us
    all_to_all x1, waiting for transfers between devices, body(): recv = lax.all_to_all(sent, SHARD, split_axis=0, concat_axis=0, tiled=True)  18.6 us
    pallas_call x7, Pallas kernels, call(): pl.pallas_call(kernel, out_shape=outs, in_specs=more.pop('in_specs', [VSP...  17.5 us
    all_gather x1, blocking collectives, body(): ups1 = lax.all_gather(up1, 'section', axis=0, tiled=True)  12.3 us
    all_gather x1, blocking collectives, body(): ups0 = lax.all_gather(up0, 'section', axis=0, tiled=True)  10.5 us
    all_to_all x1, starting transfers between devices, body(): pools = lax.all_to_all(both, SHARD, split_axis=0, concat_axis=0, tiled=True)  9.46 us
    unnamed x36, local copies, waits for them, and re-layouts  4.44 us
    ppermute x1, starting transfers between devices, body(): beside = lax.ppermute(bundle, ('section', 'core'), near_pairs)  3.95 us
  transfers between devices with their start and end apart: 6, of which 2 were waited for; matrix products, arithmetic and copies ran while one was open for 1% of the time, Pallas kernels for 5%

profile of v2, /device:TPU:1, one launch (start us, length us, event | category | flops | bytes accessed | tf_op | source)
XLA Modules:
  0.0 111.7 jit_solution(7078084696657516873)
XLA Ops:
  0.6 3.5 %pack.1 = (bf16[128,2,640]{2,1,0:T(2,128)(2,1)}, bf16[128,5376]{1,0:T(8,128)(2,1)}) custom-call(s32[2,128]{1,0:T(2,128)} %bitcast.19, s32[2,128]{1,0:T(2,128)} %bitcast.20, bf16[2,128,512]{2,1,0:T(8,128)(2,1)} %bitcast.18, bf16[128,1536]{1,0:T(8,128)(2,1)} %w_in.1, bf16[128,1536]{1,0:T(8,128)(2,1)} %w_hid.1, bf16[128,1536]{1,0:T(8,128)(2,1)} %w_qkv.1, ...), custom_call_target="tpu_custom_call" | custom-call | bytes 1640448 | tf_op jit(solution)/shard_map/pack/pallas_call | solution.py:295
  4.2 3.9 %collective-permute-start = (bf16[128,5376]{1,0:T(8,128)(2,1)}, bf16[128,5376]{1,0:T(8,128)(2,1)S(1)}, u32[]{:S(2)}, u32[]{:S(2)}) collective-permute-start(bf16[128,5376]{1,0:T(8,128)(2,1)} %get-tuple-element.18.rest_0_.refs_0_), channel_id=1, source_target_pairs={{128,0},{385,1},{256,128},{1,129},{384,256},{129,257},{0,384},{257... | collective-permute-start | bytes 4128776 | tf_op jit(solution)/shard_map/ppermute | solution.py:361
  8.1 21.3 %all-to-all-start = ((bf16[128,2,640]{2,1,0:T(2,128)(2,1)}), bf16[128,2,640]{2,1,0:T(2,128)(2,1)S(1)}, u32[]{:S(2)}, u32[]{:S(2)}) async-start(bf16[128,2,640]{2,1,0:T(2,128)(2,1)} %get-tuple-element.17), calls=%async_computation | async-start | bytes 655360 | tf_op jit(solution)/shard_map/all_to_all | solution.py:364
  29.4 0.0 copy-start.7
  29.5 3.9 %collective-permute-start.2 = (bf16[128,5376]{1,0:T(8,128)(2,1)S(1)}, bf16[128,5376]{1,0:T(8,128)(2,1)}, u32[]{:S(2)}, u32[]{:S(2)}) collective-permute-start(bf16[128,5376]{1,0:T(8,128)(2,1)S(1)} %collective-permute-done.rest_1_.refs_1_), channel_id=1, source_target_pairs={{0,1},{1,0},{2,3},{3,2},{4,5},{5,4},{6,7},{7,6},{8,9},{9,8},{10,11... | collective-permute-start | bytes 4128776 | tf_op jit(solution)/shard_map/ppermute | solution.py:366
  33.4 0.9 constant_dynamic-slice_fusion
  34.3 1.9 %collective-permute-start.1 = (bf16[64,5376]{1,0:T(8,128)(2,1)}, bf16[64,5376]{1,0:T(8,128)(2,1)}, u32[]{:S(2)}, u32[]{:S(2)}) collective-permute-start(bf16[64,5376]{1,0:T(8,128)(2,1)} %constant_dynamic-slice_fusion), channel_id=1, source_target_pairs={{128,0},{385,1},{256,128},{1,129},{384,256},{129,257},{0,384},{257... | collective-permute-start | bytes 2064392 | tf_op jit(solution)/shard_map/ppermute | solution.py:363
  36.2 18.6 %all-to-all-done.recv = bf16[128,2,640]{2,1,0:T(2,128)(2,1)S(1)} async-done(((bf16[128,2,640]{2,1,0:T(2,128)(2,1)}), bf16[128,2,640]{2,1,0:T(2,128)(2,1)S(1)}, u32[]{:S(2)}, u32[]{:S(2)}) %all-to-all-start) | async-done | bytes 327712 | tf_op jit(solution)/shard_map/all_to_all | solution.py:364
  54.8 3.7 %collective-permute-start.3 = (bf16[64,5376]{1,0:T(8,128)(2,1)}, bf16[64,5376]{1,0:T(8,128)(2,1)S(1)}, u32[]{:S(2)}, u32[]{:S(2)}) collective-permute-start(bf16[64,5376]{1,0:T(8,128)(2,1)} %collective-permute-done.1.rest_3_.refs_3_), channel_id=1, source_target_pairs={{0,1},{1,0},{2,3},{3,2},{4,5},{5,4},{6,7},{7,6},{8,9},{9,8},{10,11... | collective-permute-start | bytes 2064392 | tf_op jit(solution)/shard_map/ppermute | solution.py:368
  58.6 0.0 copy-start.5
  58.6 1.2 %copy-done.5 = bf16[1024,512]{1,0:T(8,128)(2,1)S(1)} copy-done((bf16[1024,512]{1,0:T(8,128)(2,1)S(1)}, bf16[1024,512]{1,0:T(8,128)(2,1)}, u32[]{:S(2)}) %copy-start.5) | copy-done | bytes 1048600
  59.8 0.9 fetch.1
  60.7 2.4 %first_batch.1 = (bf16[144,512]{1,0:T(8,128)(2,1)S(1)}, f32[128,1536]{1,0:T(8,128)S(1)}, bf16[512,1536]{1,0:T(8,128)(2,1)S(1)}) custom-call(bf16[128,2,640]{2,1,0:T(2,128)(2,1)S(1)} %all-to-all-done.recv, bf16[256,512]{1,0:T(8,128)(2,1)S(1)} %get-tuple-element.20.got, bf16[16,512]{1,0:T(8,128)(2,1)S(1)} %get-tuple-element.21.tail, f32[2,1536]{1,0:T(2,128)S(1)} %copy-done.7, ...), custom_call_target="tpu_custom_call" | custom-call | flops 1000000000 | bytes 6123520 | tf_op jit(solution)/shard_map/first_batch/pallas_call | solution.py:295
  63.1 10.5 %all_gather.6.ups.ups0 = bf16[576,512]{1,0:T(8,128)(2,1)S(1)} all-gather(bf16[144,512]{1,0:T(8,128)(2,1)S(1)} %get-tuple-element.25.up0), channel_id=1, replica_groups=mesh['section'=4,'chip'=64,'core'=2] {'section'}, dimensions={0}, use_global_device_ids=true | all-gather | bytes 737280 | tf_op jit(solution)/shard_map/all_gather | solution.py:388
  73.6 1.9 %second_batch.1 = (bf16[128,512]{1,0:T(8,128)(2,1)S(1)}, bf16[1024,128]{1,0:T(8,128)(2,1)}) custom-call(bf16[128,2,640]{2,1,0:T(2,128)(2,1)S(1)} %all-to-all-done.recv, bf16[256,512]{1,0:T(8,128)(2,1)S(1)} %get-tuple-element.20.got, bf16[576,512]{1,0:T(8,128)(2,1)S(1)} %all_gather.6.ups.ups0, f32[128,1536]{1,0:T(8,128)S(1)} %get-tuple-element.26.gx1, ...), custom_call_target="tpu_custom_call" | custom-call | flops 300000000 | bytes 3698688 | tf_op jit(solution)/shard_map/second_batch/pallas_call | solution.py:295
  75.5 9.5 %all-to-all-start.1 = ((bf16[128,8,128]{2,1,0:T(8,128)(2,1)}), bf16[128,8,128]{2,1,0:T(8,128)(2,1)S(1)}, u32[]{:S(2)}, u32[]{:S(2)}) async-start(bf16[128,8,128]{2,1,0:T(8,128)(2,1)} %bitcast.3), calls=%async_computation.1 | async-start | bytes 524288 | tf_op jit(solution)/shard_map/all_to_all | solution.py:397
  85.0 1.1 copy-done.2
  86.1 1.4 %place.1 = (bf16[512,1536]{1,0:T(8,128)(2,1)S(1)}, bf16[512,768]{1,0:T(8,128)(2,1)S(1)}) custom-call(bf16[128,5376]{1,0:T(8,128)(2,1)S(1)} %copy-done, bf16[128,5376]{1,0:T(8,128)(2,1)S(1)} %collective-permute-done.rest_1_.refs_1_, bf16[128,5376]{1,0:T(8,128)(2,1)} %collective-permute-done.2.rest_2_.refs_2_, ...), custom_call_target="tpu_custom_call" | custom-call | bytes 5505024 | tf_op jit(solution)/shard_map/place/pallas_call | solution.py:295
  87.5 1.2 %copy-done.8 = bf16[512,1536]{1,0:T(8,128)(2,1)} copy-done((bf16[512,1536]{1,0:T(8,128)(2,1)}, bf16[512,1536]{1,0:T(8,128)(2,1)S(1)}, u32[]{:S(2)}) %copy-start.8) | copy-done | bytes 1572888
  88.7 0.9 copy-done.10
  89.6 12.3 %all_gather.7.ups1 = bf16[512,512]{1,0:T(8,128)(2,1)S(1)} all-gather(bf16[128,512]{1,0:T(8,128)(2,1)S(1)} %get-tuple-element.28), channel_id=1, replica_groups=mesh['section'=4,'chip'=64,'core'=2] {'section'}, dimensions={0}, use_global_device_ids=true | all-gather | bytes 655360 | tf_op jit(solution)/shard_map/all_gather | solution.py:398
  101.9 3.1 %store.1 = bf16[1024,512]{1,0:T(8,128)(2,1)} custom-call(bf16[1024,512]{1,0:T(8,128)(2,1)S(1)} %copy-done.6, bf16[576,512]{1,0:T(8,128)(2,1)S(1)} %copy-done.4, bf16[512,512]{1,0:T(8,128)(2,1)S(1)} %all_gather.7.ups1), custom_call_target="tpu_custom_call" | custom-call | flops 1000000000 | bytes 2162688 | tf_op jit(solution)/shard_map/store/pallas_call | solution.py:295
  105.1 2.4 %all-to-all-done.1 = bf16[128,8,128]{2,1,0:T(8,128)(2,1)S(1)} async-done(((bf16[128,8,128]{2,1,0:T(8,128)(2,1)}), bf16[128,8,128]{2,1,0:T(8,128)(2,1)S(1)}, u32[]{:S(2)}, u32[]{:S(2)}) %all-to-all-start.1) | async-done | bytes 262176 | tf_op jit(solution)/shard_map/all_to_all | solution.py:397
  107.5 4.3 %attend.1 = bf16[2,128,512]{2,1,0:T(8,128)(2,1)} custom-call(bf16[1024,128]{1,0:T(8,128)(2,1)S(1)} %bitcast.13, s32[2,128]{1,0:T(2,128)S(1)} %copy-done.12, s32[2,10,128]{2,1,0:T(8,128)S(1)} %bitcast.14, f32[2,10,128]{2,1,0:T(8,128)S(1)} %bitcast.15, f32[1,128]{1,0:T(1,128)S(1)} %bitcast.16, f32[1,128]{1,0:T(1,128)S(1)} %bitcast.17, ...), custom_call_target="tpu_custom_call" | custom-call | flops 1000000000 | bytes 2643968 | tf_op jit(solution)/shard_map/attend/pallas_call | solution.py:295
  (34 shorter events, 0.1 us)
Async XLA Ops:
  4.2 25.3 %collective-permute-start = (bf16[128,5376]{1,0:T(8,128)(2,1)}, bf16[128,5376]{1,0:T(8,128)(2,1)S(1)}, u32[]{:S(2)}, u32[]{:S(2)}) collective-permute-start(bf16[128,5376]{1,0:T(8,128)(2,1)} %get-tuple-element.18.rest_0_.refs_0_), channel_id=1, source_target_pairs={{128,0},{385,1},{256,128},{1,129},{384,256},{129,257},{0,384},{257... | collective-permute-start | bytes 4128776 | tf_op jit(solution)/shard_map/ppermute | solution.py:361
  8.1 46.7 %all-to-all-start = ((bf16[128,2,640]{2,1,0:T(2,128)(2,1)}), bf16[128,2,640]{2,1,0:T(2,128)(2,1)S(1)}, u32[]{:S(2)}, u32[]{:S(2)}) async-start(bf16[128,2,640]{2,1,0:T(2,128)(2,1)} %get-tuple-element.17), calls=%async_computation | async-start | bytes 655360 | tf_op jit(solution)/shard_map/all_to_all | solution.py:364
  29.4 31.3 %copy-start.7 = (f32[2,1536]{1,0:T(2,128)S(1)}, f32[2,1536]{1,0:T(2,128)}, u32[]{:S(2)}) copy-start(f32[2,1536]{1,0:T(2,128)} %bias.3) | copy-start | bytes 36868
  29.4 31.3 %copy-start = (bf16[128,5376]{1,0:T(8,128)(2,1)S(1)}, bf16[128,5376]{1,0:T(8,128)(2,1)}, u32[]{:S(2)}) copy-start(bf16[128,5376]{1,0:T(8,128)(2,1)} %get-tuple-element.18.rest_0_.refs_0_) | copy-start | bytes 4128772
  29.5 25.4 %collective-permute-start.2 = (bf16[128,5376]{1,0:T(8,128)(2,1)S(1)}, bf16[128,5376]{1,0:T(8,128)(2,1)}, u32[]{:S(2)}, u32[]{:S(2)}) collective-permute-start(bf16[128,5376]{1,0:T(8,128)(2,1)S(1)} %collective-permute-done.rest_1_.refs_1_), channel_id=1, source_target_pairs={{0,1},{1,0},{2,3},{3,2},{4,5},{5,4},{6,7},{7,6},{8,9},{9,8},{10,11... | collective-permute-start | bytes 4128776 | tf_op jit(solution)/shard_map/ppermute | solution.py:366
  34.3 20.6 %collective-permute-start.1 = (bf16[64,5376]{1,0:T(8,128)(2,1)}, bf16[64,5376]{1,0:T(8,128)(2,1)}, u32[]{:S(2)}, u32[]{:S(2)}) collective-permute-start(bf16[64,5376]{1,0:T(8,128)(2,1)} %constant_dynamic-slice_fusion), channel_id=1, source_target_pairs={{128,0},{385,1},{256,128},{1,129},{384,256},{129,257},{0,384},{257... | collective-permute-start | bytes 2064392 | tf_op jit(solution)/shard_map/ppermute | solution.py:363
  54.8 5.8 %collective-permute-start.3 = (bf16[64,5376]{1,0:T(8,128)(2,1)}, bf16[64,5376]{1,0:T(8,128)(2,1)S(1)}, u32[]{:S(2)}, u32[]{:S(2)}) collective-permute-start(bf16[64,5376]{1,0:T(8,128)(2,1)} %collective-permute-done.1.rest_3_.refs_3_), channel_id=1, source_target_pairs={{0,1},{1,0},{2,3},{3,2},{4,5},{5,4},{6,7},{7,6},{8,9},{9,8},{10,11... | collective-permute-start | bytes 2064392 | tf_op jit(solution)/shard_map/ppermute | solution.py:368
  58.6 1.2 %copy-start.5 = (bf16[1024,512]{1,0:T(8,128)(2,1)S(1)}, bf16[1024,512]{1,0:T(8,128)(2,1)}, u32[]{:S(2)}) copy-start(bf16[1024,512]{1,0:T(8,128)(2,1)} %memory.3) | copy-start | bytes 3145732
  60.7 2.4 %copy-start.1 = (bf16[64,5376]{1,0:T(8,128)(2,1)}, bf16[64,5376]{1,0:T(8,128)(2,1)S(1)}, u32[]{:S(2)}) copy-start(bf16[64,5376]{1,0:T(8,128)(2,1)S(1)} %collective-permute-done.3.rest_4_.refs_4_) | copy-start | bytes 2064388
  73.6 1.9 %copy-start.3 = (bf16[576,512]{1,0:T(8,128)(2,1)}, bf16[576,512]{1,0:T(8,128)(2,1)S(1)}, u32[]{:S(2)}) copy-start(bf16[576,512]{1,0:T(8,128)(2,1)S(1)} %all_gather.6.ups.ups0) | copy-start | bytes 1769476
  73.6 11.3 %copy-start.15 = (s32[2,128,10]{1,0,2:T(2,128)S(1)}, s32[2,128,10]{1,0,2:T(2,128)}, u32[]{:S(2)}) copy-start(s32[2,128,10]{1,0,2:T(2,128)} %param.20) | copy-start | bytes 30724
  73.6 11.4 %copy-start.16 = (f32[2,128,10]{1,0,2:T(2,128)S(1)}, f32[2,128,10]{1,0,2:T(2,128)}, u32[]{:S(2)}) copy-start(f32[2,128,10]{1,0,2:T(2,128)} %param.21) | copy-start | bytes 30724
  75.5 32.0 %all-to-all-start.1 = ((bf16[128,8,128]{2,1,0:T(8,128)(2,1)}), bf16[128,8,128]{2,1,0:T(8,128)(2,1)S(1)}, u32[]{:S(2)}, u32[]{:S(2)}) async-start(bf16[128,8,128]{2,1,0:T(8,128)(2,1)} %bitcast.3), calls=%async_computation.1 | async-start | bytes 524288 | tf_op jit(solution)/shard_map/all_to_all | solution.py:397
  85.0 1.1 copy-start.2
  86.1 15.8 %copy-start.4 = (bf16[576,512]{1,0:T(8,128)(2,1)S(1)}, bf16[576,512]{1,0:T(8,128)(2,1)}, u32[]{:S(2)}) copy-start(bf16[576,512]{1,0:T(8,128)(2,1)} %copy-done.3) | copy-start | bytes 1769476
  86.1 15.8 %copy-start.6 = (bf16[1024,512]{1,0:T(8,128)(2,1)S(1)}, bf16[1024,512]{1,0:T(8,128)(2,1)}, u32[]{:S(2)}) copy-start(bf16[1024,512]{1,0:T(8,128)(2,1)} %memory.3) | copy-start | bytes 3145732
  87.5 1.2 %copy-start.8 = (bf16[512,1536]{1,0:T(8,128)(2,1)}, bf16[512,1536]{1,0:T(8,128)(2,1)S(1)}, u32[]{:S(2)}) copy-start(bf16[512,1536]{1,0:T(8,128)(2,1)S(1)} %get-tuple-element.30.w) | copy-start | bytes 4718596
  88.7 0.9 copy-start.10
  101.9 5.5 %copy-start.9 = (bf16[512,1536]{1,0:T(8,128)(2,1)S(1)}, bf16[512,1536]{1,0:T(8,128)(2,1)}, u32[]{:S(2)}) copy-start(bf16[512,1536]{1,0:T(8,128)(2,1)} %copy-done.8) | copy-start | bytes 4718596
  101.9 5.5 %copy-start.11 = (bf16[512,768]{1,0:T(8,128)(2,1)S(1)}, bf16[512,768]{1,0:T(8,128)(2,1)}, u32[]{:S(2)}) copy-start(bf16[512,768]{1,0:T(8,128)(2,1)} %copy-done.10) | copy-start | bytes 2359300
  101.9 5.5 %copy-start.12 = (s32[2,128]{1,0:T(2,128)S(1)}, s32[2,128]{1,0:T(2,128)}, u32[]{:S(2)}) copy-start(s32[2,128]{1,0:T(2,128)} %source.1) | copy-start | bytes 3076
  101.9 5.5 %copy-start.13 = (f32[128]{0:T(128)S(1)}, f32[128]{0:T(128)}, u32[]{:S(2)}) copy-start(f32[128]{0:T(128)} %param.22) | copy-start | bytes 1540
  101.9 5.5 %copy-start.14 = (f32[128]{0:T(128)S(1)}, f32[128]{0:T(128)}, u32[]{:S(2)}) copy-start(f32[128]{0:T(128)} %param.23) | copy-start | bytes 1540

commit v3 on v2

--- a/solution.py
+++ b/solution.py
@@ -138,24 +138,19 @@
     return ((1.0 - update) * fresh + update * h.astype(F32)).astype(BF)
 
 
-def fetch_kernel(recv, memory, got, tail):
+def first_kernel(recv, memory, bias, *rest):
+    pieces, (up, got, gx1, w_hid, w_in, sems) = rest[:5], rest[5:]
+    in_copies = copies(pieces, 0, G, w_in, sems.at[0])
+    hid_copies = copies(pieces, G, G, w_hid, sems.at[1])
     slots = recv.shape[0]
     rows = memory.shape[0]
     digits = recv[:, 0, F:].astype(F32)
-    tail[...] = jnp.zeros((EXTRA, F), BF)
-    tail[:, :slots] = digits.T[:EXTRA, :].astype(BF)
+    up[slots:, :] = jnp.zeros((EXTRA, F), BF)
+    up[slots:, :slots] = digits.T[:EXTRA, :].astype(BF)
     number = iota((slots, rows), 1).astype(F32)
     hot0 = hot(number == digits[:, 0:1] * DIGIT + digits[:, 1:2])
     hot1 = hot(number == digits[:, 2:3] * DIGIT + digits[:, 3:4])
     got[...] = dot(jnp.concatenate([hot0, hot1], axis=0), memory[...]).astype(BF)
-
-
-def first_kernel(recv, got, tail, bias, *rest):
-    pieces, (up, gx1, w_hid, w_in, sems) = rest[:5], rest[5:]
-    in_copies = copies(pieces, 0, G, w_in, sems.at[0])
-    hid_copies = copies(pieces, G, G, w_hid, sems.at[1])
-    slots = recv.shape[0]
-    up[slots:, :] = tail[...]
     sent = jnp.concatenate([recv[:, b, :F] for b in range(BATCHES)], axis=0)
     wait(in_copies)
     gx = dot(sent, w_in[...]) + bias[0:1, :]
@@ -367,22 +362,19 @@
     recv, beside, far, across = lax.optimization_barrier((recv, beside, far, across))
     far_across = lax.ppermute(far, "core", swap)
     pieces = (bundle, beside, across, far, far_across)
-    got, tail = call(
-        fetch_kernel,
-        2,
-        [shape((2 * slots, F), BF), shape((EXTRA, F), BF)],
-        3 * 10**8,
-        (recv, memory),
-        "fetch",
-    )
-    up0, gx1, w_hid = call(
+    up0, got, gx1, w_hid = call(
         first_kernel,
-        9,
-        [shape((slots + EXTRA, F), BF), shape((slots, G), F32), shape((F, G), BF)],
+        8,
+        [
+            shape((slots + EXTRA, F), BF),
+            shape((2 * slots, F), BF),
+            shape((slots, G), F32),
+            shape((F, G), BF),
+        ],
         10**9,
-        (recv, got, tail, gru_bias) + pieces,
+        (recv, memory, gru_bias) + pieces,
         "first_batch",
-        in_specs=[VSPEC] * 4 + [HSPEC] * 5,
+        in_specs=[VSPEC] * 3 + [HSPEC] * 5,
         scratch_shapes=[pltpu.VMEM((F, G), BF), pltpu.SemaphoreType.DMA((2, 5))],
     )
     ups0 = lax.all_gather(up0, "section", axis=0, tiled=True)

time: 114 us -> 115 us (level)
  waiting for transfers between devices: 21 us -> 22.9 us
    ppermute x1, waiting for transfers between devices: 0.01 us -> 1.96 us  [body(): far_across = lax.ppermute(far, 'core', swap)]
    pallas_call x7 -> x6, Pallas kernels: 17.5 us -> 16.9 us  [call(): pl.pallas_call(kernel, out_shape=outs, in_specs=more.pop('in_specs', [VSP...]
  transfers between devices with their start and end apart: 6 -> 6, of which waited for: 2 -> 3; matrix products, arithmetic and copies ran while one was open for 1% -> 1% of each run, Pallas kernels for 5% -> 4%
where the time goes in v3:
time: 115 us; the launch traced here: 113 us
  starting transfers between devices  45 us (39%)
  waiting for transfers between devices  22.9 us (20%)
  blocking collectives  22.4 us (19%)
  Pallas kernels  16.9 us (15%)
  local copies, waits for them, and re-layouts  5.34 us (5%)
    all_to_all x1, starting transfers between devices, body(): recv = lax.all_to_all(sent, SHARD, split_axis=0, concat_axis=0, tiled=True)  21.3 us
    all_to_all x1, waiting for transfers between devices, body(): recv = lax.all_to_all(sent, SHARD, split_axis=0, concat_axis=0, tiled=True)  18.6 us
    pallas_call x6, Pallas kernels, call(): pl.pallas_call(kernel, out_shape=outs, in_specs=more.pop('in_specs', [VSP...  16.9 us
    all_gather x1, blocking collectives, body(): ups1 = lax.all_gather(up1, 'section', axis=0, tiled=True)  12.3 us
    all_to_all x1, starting transfers between devices, body(): pools = lax.all_to_all(both, SHARD, split_axis=0, concat_axis=0, tiled=True)  10.1 us
    all_gather x1, blocking collectives, body(): ups0 = lax.all_gather(up0, 'section', axis=0, tiled=True)  10 us
    unnamed x36, local copies, waits for them, and re-layouts  4.44 us
    ppermute x1, starting transfers between devices, body(): beside = lax.ppermute(bundle, ('section', 'core'), near_pairs)  4.08 us
  transfers between devices with their start and end apart: 6, of which 3 were waited for; matrix products, arithmetic and copies ran while one was open for 1% of the time, Pallas kernels for 4%

profile of v3, /device:TPU:1, one launch (start us, length us, event | category | flops | bytes accessed | tf_op | source)
XLA Modules:
  0.0 113.5 jit_solution(520194515467599678)
XLA Ops:
  0.6 3.5 %pack.1 = (bf16[128,2,640]{2,1,0:T(2,128)(2,1)}, bf16[128,5376]{1,0:T(8,128)(2,1)}) custom-call(s32[2,128]{1,0:T(2,128)} %bitcast.19, s32[2,128]{1,0:T(2,128)} %bitcast.20, bf16[2,128,512]{2,1,0:T(8,128)(2,1)} %bitcast.18, bf16[128,1536]{1,0:T(8,128)(2,1)} %w_in.1, bf16[128,1536]{1,0:T(8,128)(2,1)} %w_hid.1, bf16[128,1536]{1,0:T(8,128)(2,1)} %w_qkv.1, ...), custom_call_target="tpu_custom_call" | custom-call | bytes 1640448 | tf_op jit(solution)/shard_map/pack/pallas_call | solution.py:290
  4.2 0.0 copy-start.7
  4.2 4.1 %collective-permute-start = (bf16[128,5376]{1,0:T(8,128)(2,1)}, bf16[128,5376]{1,0:T(8,128)(2,1)S(1)}, u32[]{:S(2)}, u32[]{:S(2)}) collective-permute-start(bf16[128,5376]{1,0:T(8,128)(2,1)} %get-tuple-element.17.rest_0_.refs_0_), channel_id=1, source_target_pairs={{128,0},{385,1},{256,128},{1,129},{384,256},{129,257},{0,384},{257... | collective-permute-start | bytes 4128776 | tf_op jit(solution)/shard_map/ppermute | solution.py:356
  8.3 21.3 %all-to-all-start = ((bf16[128,2,640]{2,1,0:T(2,128)(2,1)}), bf16[128,2,640]{2,1,0:T(2,128)(2,1)S(1)}, u32[]{:S(2)}, u32[]{:S(2)}) async-start(bf16[128,2,640]{2,1,0:T(2,128)(2,1)} %get-tuple-element.16), calls=%async_computation | async-start | bytes 655360 | tf_op jit(solution)/shard_map/all_to_all | solution.py:359
  29.6 3.9 %collective-permute-start.2 = (bf16[128,5376]{1,0:T(8,128)(2,1)S(1)}, bf16[128,5376]{1,0:T(8,128)(2,1)}, u32[]{:S(2)}, u32[]{:S(2)}) collective-permute-start(bf16[128,5376]{1,0:T(8,128)(2,1)S(1)} %collective-permute-done.rest_1_.refs_1_), channel_id=1, source_target_pairs={{0,1},{1,0},{2,3},{3,2},{4,5},{5,4},{6,7},{7,6},{8,9},{9,8},{10,11... | collective-permute-start | bytes 4128776 | tf_op jit(solution)/shard_map/ppermute | solution.py:361
  33.5 0.9 constant_dynamic-slice_fusion
  34.4 1.9 %collective-permute-start.1 = (bf16[64,5376]{1,0:T(8,128)(2,1)}, bf16[64,5376]{1,0:T(8,128)(2,1)}, u32[]{:S(2)}, u32[]{:S(2)}) collective-permute-start(bf16[64,5376]{1,0:T(8,128)(2,1)} %constant_dynamic-slice_fusion), channel_id=1, source_target_pairs={{128,0},{385,1},{256,128},{1,129},{384,256},{129,257},{0,384},{257... | collective-permute-start | bytes 2064392 | tf_op jit(solution)/shard_map/ppermute | solution.py:358
  36.3 18.6 %all-to-all-done.recv = bf16[128,2,640]{2,1,0:T(2,128)(2,1)S(1)} async-done(((bf16[128,2,640]{2,1,0:T(2,128)(2,1)}), bf16[128,2,640]{2,1,0:T(2,128)(2,1)S(1)}, u32[]{:S(2)}, u32[]{:S(2)}) %all-to-all-start) | async-done | bytes 327712 | tf_op jit(solution)/shard_map/all_to_all | solution.py:359
  55.0 3.7 %collective-permute-start.3 = (bf16[64,5376]{1,0:T(8,128)(2,1)}, bf16[64,5376]{1,0:T(8,128)(2,1)S(1)}, u32[]{:S(2)}, u32[]{:S(2)}) collective-permute-start(bf16[64,5376]{1,0:T(8,128)(2,1)} %collective-permute-done.1.rest_3_.refs_3_), channel_id=1, source_target_pairs={{0,1},{1,0},{2,3},{3,2},{4,5},{5,4},{6,7},{7,6},{8,9},{9,8},{10,11... | collective-permute-start | bytes 2064392 | tf_op jit(solution)/shard_map/ppermute | solution.py:363
  58.7 2.0 %collective-permute-done.3.rest_4_.refs_4_ = bf16[64,5376]{1,0:T(8,128)(2,1)S(1)} collective-permute-done((bf16[64,5376]{1,0:T(8,128)(2,1)}, bf16[64,5376]{1,0:T(8,128)(2,1)S(1)}, u32[]{:S(2)}, u32[]{:S(2)}) %collective-permute-start.3) | collective-permute-done | bytes 688160 | tf_op jit(solution)/shard_map/ppermute | solution.py:363
  60.7 1.2 %copy-done.5 = bf16[1024,512]{1,0:T(8,128)(2,1)S(1)} copy-done((bf16[1024,512]{1,0:T(8,128)(2,1)S(1)}, bf16[1024,512]{1,0:T(8,128)(2,1)}, u32[]{:S(2)}) %copy-start.5) | copy-done | bytes 1048600
  61.9 2.7 %first_batch.1 = (bf16[144,512]{1,0:T(8,128)(2,1)S(1)}, bf16[256,512]{1,0:T(8,128)(2,1)S(1)}, f32[128,1536]{1,0:T(8,128)S(1)}, bf16[512,1536]{1,0:T(8,128)(2,1)S(1)}) custom-call(bf16[128,2,640]{2,1,0:T(2,128)(2,1)S(1)} %all-to-all-done.recv, bf16[1024,512]{1,0:T(8,128)(2,1)S(1)} %copy-done.5, f32[2,1536]{1,0:T(2,128)S(1)} %copy-done.7, ...), custom_call_target="tpu_custom_call" | custom-call | flops 1000000000 | bytes 6893568 | tf_op jit(solution)/shard_map/first_batch/pallas_call | solution.py:290
  64.6 10.0 %all_gather.6.ups.ups0 = bf16[576,512]{1,0:T(8,128)(2,1)S(1)} all-gather(bf16[144,512]{1,0:T(8,128)(2,1)S(1)} %get-tuple-element.22.up0), channel_id=1, replica_groups=mesh['section'=4,'chip'=64,'core'=2] {'section'}, dimensions={0}, use_global_device_ids=true | all-gather | bytes 737280 | tf_op jit(solution)/shard_map/all_gather | solution.py:380
  74.7 1.9 %second_batch.1 = (bf16[128,512]{1,0:T(8,128)(2,1)S(1)}, bf16[1024,128]{1,0:T(8,128)(2,1)}) custom-call(bf16[128,2,640]{2,1,0:T(2,128)(2,1)S(1)} %all-to-all-done.recv, bf16[256,512]{1,0:T(8,128)(2,1)S(1)} %get-tuple-element.23.got, bf16[576,512]{1,0:T(8,128)(2,1)S(1)} %all_gather.6.ups.ups0, f32[128,1536]{1,0:T(8,128)S(1)} %get-tuple-element.24.gx1, ...), custom_call_target="tpu_custom_call" | custom-call | flops 300000000 | bytes 3698688 | tf_op jit(solution)/shard_map/second_batch/pallas_call | solution.py:290
  76.5 10.1 %all-to-all-start.1 = ((bf16[128,8,128]{2,1,0:T(8,128)(2,1)}), bf16[128,8,128]{2,1,0:T(8,128)(2,1)S(1)}, u32[]{:S(2)}, u32[]{:S(2)}) async-start(bf16[128,8,128]{2,1,0:T(8,128)(2,1)} %bitcast.3), calls=%async_computation.1 | async-start | bytes 524288 | tf_op jit(solution)/shard_map/all_to_all | solution.py:389
  86.7 1.1 copy-done.2
  87.8 1.4 %place.1 = (bf16[512,1536]{1,0:T(8,128)(2,1)S(1)}, bf16[512,768]{1,0:T(8,128)(2,1)S(1)}) custom-call(bf16[128,5376]{1,0:T(8,128)(2,1)S(1)} %copy-done, bf16[128,5376]{1,0:T(8,128)(2,1)S(1)} %collective-permute-done.rest_1_.refs_1_, bf16[128,5376]{1,0:T(8,128)(2,1)} %collective-permute-done.2.rest_2_.refs_2_, ...), custom_call_target="tpu_custom_call" | custom-call | bytes 5505024 | tf_op jit(solution)/shard_map/place/pallas_call | solution.py:290
  89.3 1.2 %copy-done.8 = bf16[512,1536]{1,0:T(8,128)(2,1)} copy-done((bf16[512,1536]{1,0:T(8,128)(2,1)}, bf16[512,1536]{1,0:T(8,128)(2,1)S(1)}, u32[]{:S(2)}) %copy-start.8) | copy-done | bytes 1572888
  90.4 0.9 copy-done.10
  91.3 12.3 %all_gather.7.ups1 = bf16[512,512]{1,0:T(8,128)(2,1)S(1)} all-gather(bf16[128,512]{1,0:T(8,128)(2,1)S(1)} %get-tuple-element.26), channel_id=1, replica_groups=mesh['section'=4,'chip'=64,'core'=2] {'section'}, dimensions={0}, use_global_device_ids=true | all-gather | bytes 655360 | tf_op jit(solution)/shard_map/all_gather | solution.py:390
  103.7 0.0 copy-start.14
  103.7 3.1 %store.1 = bf16[1024,512]{1,0:T(8,128)(2,1)} custom-call(bf16[1024,512]{1,0:T(8,128)(2,1)S(1)} %copy-done.6, bf16[576,512]{1,0:T(8,128)(2,1)S(1)} %copy-done.4, bf16[512,512]{1,0:T(8,128)(2,1)S(1)} %all_gather.7.ups1), custom_call_target="tpu_custom_call" | custom-call | flops 1000000000 | bytes 2162688 | tf_op jit(solution)/shard_map/store/pallas_call | solution.py:290
  106.9 2.3 %all-to-all-done.1 = bf16[128,8,128]{2,1,0:T(8,128)(2,1)S(1)} async-done(((bf16[128,8,128]{2,1,0:T(8,128)(2,1)}), bf16[128,8,128]{2,1,0:T(8,128)(2,1)S(1)}, u32[]{:S(2)}, u32[]{:S(2)}) %all-to-all-start.1) | async-done | bytes 262176 | tf_op jit(solution)/shard_map/all_to_all | solution.py:389
  109.2 4.3 %attend.1 = bf16[2,128,512]{2,1,0:T(8,128)(2,1)} custom-call(bf16[1024,128]{1,0:T(8,128)(2,1)S(1)} %bitcast.13, s32[2,128]{1,0:T(2,128)S(1)} %copy-done.12, s32[2,10,128]{2,1,0:T(8,128)S(1)} %bitcast.14, f32[2,10,128]{2,1,0:T(8,128)S(1)} %bitcast.15, f32[1,128]{1,0:T(1,128)S(1)} %bitcast.16, f32[1,128]{1,0:T(1,128)S(1)} %bitcast.17, ...), custom_call_target="tpu_custom_call" | custom-call | flops 1000000000 | bytes 2643968 | tf_op jit(solution)/shard_map/attend/pallas_call | solution.py:290
  (33 shorter events, 0.1 us)
Async XLA Ops:
  4.2 56.5 %copy-start = (bf16[128,5376]{1,0:T(8,128)(2,1)S(1)}, bf16[128,5376]{1,0:T(8,128)(2,1)}, u32[]{:S(2)}) copy-start(bf16[128,5376]{1,0:T(8,128)(2,1)} %get-tuple-element.17.rest_0_.refs_0_) | copy-start | bytes 4128772
  4.2 56.5 %copy-start.7 = (f32[2,1536]{1,0:T(2,128)S(1)}, f32[2,1536]{1,0:T(2,128)}, u32[]{:S(2)}) copy-start(f32[2,1536]{1,0:T(2,128)} %bias.3) | copy-start | bytes 36868
  4.2 25.4 %collective-permute-start = (bf16[128,5376]{1,0:T(8,128)(2,1)}, bf16[128,5376]{1,0:T(8,128)(2,1)S(1)}, u32[]{:S(2)}, u32[]{:S(2)}) collective-permute-start(bf16[128,5376]{1,0:T(8,128)(2,1)} %get-tuple-element.17.rest_0_.refs_0_), channel_id=1, source_target_pairs={{128,0},{385,1},{256,128},{1,129},{384,256},{129,257},{0,384},{257... | collective-permute-start | bytes 4128776 | tf_op jit(solution)/shard_map/ppermute | solution.py:356
  8.3 46.7 %all-to-all-start = ((bf16[128,2,640]{2,1,0:T(2,128)(2,1)}), bf16[128,2,640]{2,1,0:T(2,128)(2,1)S(1)}, u32[]{:S(2)}, u32[]{:S(2)}) async-start(bf16[128,2,640]{2,1,0:T(2,128)(2,1)} %get-tuple-element.16), calls=%async_computation | async-start | bytes 655360 | tf_op jit(solution)/shard_map/all_to_all | solution.py:359
  29.6 25.4 %collective-permute-start.2 = (bf16[128,5376]{1,0:T(8,128)(2,1)S(1)}, bf16[128,5376]{1,0:T(8,128)(2,1)}, u32[]{:S(2)}, u32[]{:S(2)}) collective-permute-start(bf16[128,5376]{1,0:T(8,128)(2,1)S(1)} %collective-permute-done.rest_1_.refs_1_), channel_id=1, source_target_pairs={{0,1},{1,0},{2,3},{3,2},{4,5},{5,4},{6,7},{7,6},{8,9},{9,8},{10,11... | collective-permute-start | bytes 4128776 | tf_op jit(solution)/shard_map/ppermute | solution.py:361
  34.4 20.6 %collective-permute-start.1 = (bf16[64,5376]{1,0:T(8,128)(2,1)}, bf16[64,5376]{1,0:T(8,128)(2,1)}, u32[]{:S(2)}, u32[]{:S(2)}) collective-permute-start(bf16[64,5376]{1,0:T(8,128)(2,1)} %constant_dynamic-slice_fusion), channel_id=1, source_target_pairs={{128,0},{385,1},{256,128},{1,129},{384,256},{129,257},{0,384},{257... | collective-permute-start | bytes 2064392 | tf_op jit(solution)/shard_map/ppermute | solution.py:358
  55.0 5.7 %collective-permute-start.3 = (bf16[64,5376]{1,0:T(8,128)(2,1)}, bf16[64,5376]{1,0:T(8,128)(2,1)S(1)}, u32[]{:S(2)}, u32[]{:S(2)}) collective-permute-start(bf16[64,5376]{1,0:T(8,128)(2,1)} %collective-permute-done.1.rest_3_.refs_3_), channel_id=1, source_target_pairs={{0,1},{1,0},{2,3},{3,2},{4,5},{5,4},{6,7},{7,6},{8,9},{9,8},{10,11... | collective-permute-start | bytes 2064392 | tf_op jit(solution)/shard_map/ppermute | solution.py:363
  60.7 1.2 %copy-start.5 = (bf16[1024,512]{1,0:T(8,128)(2,1)S(1)}, bf16[1024,512]{1,0:T(8,128)(2,1)}, u32[]{:S(2)}) copy-start(bf16[1024,512]{1,0:T(8,128)(2,1)} %memory.3) | copy-start | bytes 3145732
  61.9 2.7 %copy-start.1 = (bf16[64,5376]{1,0:T(8,128)(2,1)}, bf16[64,5376]{1,0:T(8,128)(2,1)S(1)}, u32[]{:S(2)}) copy-start(bf16[64,5376]{1,0:T(8,128)(2,1)S(1)} %collective-permute-done.3.rest_4_.refs_4_) | copy-start | bytes 2064388
  74.7 1.9 %copy-start.3 = (bf16[576,512]{1,0:T(8,128)(2,1)}, bf16[576,512]{1,0:T(8,128)(2,1)S(1)}, u32[]{:S(2)}) copy-start(bf16[576,512]{1,0:T(8,128)(2,1)S(1)} %all_gather.6.ups.ups0) | copy-start | bytes 1769476
  74.7 12.0 %copy-start.15 = (s32[2,128,10]{1,0,2:T(2,128)S(1)}, s32[2,128,10]{1,0,2:T(2,128)}, u32[]{:S(2)}) copy-start(s32[2,128,10]{1,0,2:T(2,128)} %param.20) | copy-start | bytes 30724
  74.7 12.0 %copy-start.16 = (f32[2,128,10]{1,0,2:T(2,128)S(1)}, f32[2,128,10]{1,0,2:T(2,128)}, u32[]{:S(2)}) copy-start(f32[2,128,10]{1,0,2:T(2,128)} %param.21) | copy-start | bytes 30724
  76.5 32.6 %all-to-all-start.1 = ((bf16[128,8,128]{2,1,0:T(8,128)(2,1)}), bf16[128,8,128]{2,1,0:T(8,128)(2,1)S(1)}, u32[]{:S(2)}, u32[]{:S(2)}) async-start(bf16[128,8,128]{2,1,0:T(8,128)(2,1)} %bitcast.3), calls=%async_computation.1 | async-start | bytes 524288 | tf_op jit(solution)/shard_map/all_to_all | solution.py:389
  86.7 1.1 copy-start.2
  87.8 15.8 %copy-start.4 = (bf16[576,512]{1,0:T(8,128)(2,1)S(1)}, bf16[576,512]{1,0:T(8,128)(2,1)}, u32[]{:S(2)}) copy-start(bf16[576,512]{1,0:T(8,128)(2,1)} %copy-done.3) | copy-start | bytes 1769476
  87.8 15.8 %copy-start.6 = (bf16[1024,512]{1,0:T(8,128)(2,1)S(1)}, bf16[1024,512]{1,0:T(8,128)(2,1)}, u32[]{:S(2)}) copy-start(bf16[1024,512]{1,0:T(8,128)(2,1)} %memory.3) | copy-start | bytes 3145732
  89.3 1.2 %copy-start.8 = (bf16[512,1536]{1,0:T(8,128)(2,1)}, bf16[512,1536]{1,0:T(8,128)(2,1)S(1)}, u32[]{:S(2)}) copy-start(bf16[512,1536]{1,0:T(8,128)(2,1)S(1)} %get-tuple-element.28.w) | copy-start | bytes 4718596
  90.4 0.9 copy-start.10
  103.7 5.5 %copy-start.9 = (bf16[512,1536]{1,0:T(8,128)(2,1)S(1)}, bf16[512,1536]{1,0:T(8,128)(2,1)}, u32[]{:S(2)}) copy-start(bf16[512,1536]{1,0:T(8,128)(2,1)} %copy-done.8) | copy-start | bytes 4718596
  103.7 5.5 %copy-start.11 = (bf16[512,768]{1,0:T(8,128)(2,1)S(1)}, bf16[512,768]{1,0:T(8,128)(2,1)}, u32[]{:S(2)}) copy-start(bf16[512,768]{1,0:T(8,128)(2,1)} %copy-done.10) | copy-start | bytes 2359300
  103.7 5.5 %copy-start.12 = (s32[2,128]{1,0:T(2,128)S(1)}, s32[2,128]{1,0:T(2,128)}, u32[]{:S(2)}) copy-start(s32[2,128]{1,0:T(2,128)} %source.1) | copy-start | bytes 3076
  103.7 5.5 %copy-start.13 = (f32[128]{0:T(128)S(1)}, f32[128]{0:T(128)}, u32[]{:S(2)}) copy-start(f32[128]{0:T(128)} %param.22) | copy-start | bytes 1540
  103.7 5.5 %copy-start.14 = (f32[128]{0:T(128)S(1)}, f32[128]{0:T(128)}, u32[]{:S(2)}) copy-start(f32[128]{0:T(128)} %param.23) | copy-start | bytes 1540
